TPU v7x, 32 devices: a whole 2x2x4 slice. The times are simulated.
32 devices in a mesh: dp: 16 (over z, y, x), rep: 2 (over core).
Axes of the slice: x: 2, y: 2, z: 4, core: 2. Of those that a mesh axis runs over, the one named last changes fastest.
Arguments:
- media: bfloat16 [32, 5, 256, 1024], P(('dp', 'rep')), may hold values from -6 to 6
- latents: bfloat16 [32, 5, 64, 1024], P(('dp', 'rep')), may hold values from -6 to 6
- image_counts: int32 [32], P(('dp', 'rep')), may hold values from 1 to 5, as said below
- grad_out: bfloat16 [32, 5, 64, 1024], P(('dp', 'rep')), may hold values from -6 to 6
- media_gain: bfloat16 [1024], P('dp'), may hold values from 0.25 to 1.75
- media_bias: bfloat16 [1024], P('dp'), may hold values from -3 to 3
- latent_gain: bfloat16 [1024], P('dp'), may hold values from 0.25 to 1.75
- latent_bias: bfloat16 [1024], P('dp'), may hold values from -3 to 3
- feed_gain: bfloat16 [1024], P('dp'), may hold values from 0.25 to 1.75
- feed_bias: bfloat16 [1024], P('dp'), may hold values from -3 to 3
- query_weight: bfloat16 [1024, 512], P('dp'), may hold values from -0.1875 to 0.1875
- context_weight: bfloat16 [1024, 1024], P('dp'), may hold values from -0.1875 to 0.1875
- output_weight: bfloat16 [512, 1024], P('dp'), may hold values from -1.5 to 1.5
- up_weight: bfloat16 [1024, 4096], P('dp'), may hold values from -0.1875 to 0.1875
- down_weight: bfloat16 [4096, 1024], P('dp'), may hold values from -0.09375 to 0.09375
Outputs:
- latents_out: bfloat16 [32, 5, 64, 1024], P(('dp', 'rep'))
- grad_media: bfloat16 [32, 5, 256, 1024], P(('dp', 'rep'))
- grad_latents: bfloat16 [32, 5, 64, 1024], P(('dp', 'rep'))
- grad_media_gain: float32 [1024], P('dp')
- grad_media_bias: float32 [1024], P('dp')
- grad_latent_gain: float32 [1024], P('dp')
- grad_latent_bias: float32 [1024], P('dp')
- grad_feed_gain: float32 [1024], P('dp')
- grad_feed_bias: float32 [1024], P('dp')
- grad_query: float32 [1024, 512], P('dp')
- grad_context: float32 [1024, 1024], P('dp')
- grad_output: float32 [512, 1024], P('dp')
- grad_up: float32 [1024, 4096], P('dp')
- grad_down: float32 [4096, 1024], P('dp')
Inputs may be any that keep to these rules, and one draw needn't show every extreme that they name: Slot j of sample s holds an image where j < image_counts[s]; the other slots are empty. Some sample holds 5 images and some holds one.
All inputs are finite; a program needn't handle non-finite values.
Results may differ from a plain program's by a relative error of at most 0.014.
Values may be sent and summed in bfloat16 or wider, within the bound.
A program may use at most 192 MiB of HBM per device.

v0:
```python
import functools

import jax
import jax.numpy as jnp
from jax import lax
from jax.experimental import pallas as pl
from jax.experimental.pallas import tpu as pltpu
from jax.sharding import PartitionSpec as P

HEAD_DIM = 64
GROUP = 256

epsilon = 1e-05

MESH = pl.DeviceIdType.MESH
ALL = slice(None)
F32 = jnp.float32
BF16 = jnp.bfloat16


class Links:
    def __init__(self, length):
        self.length = length
        self.dp = lax.axis_index("dp")
        self.rep = lax.axis_index("rep")
        self.z = lax.div(self.dp, 4)
        self.y = lax.rem(lax.div(self.dp, 2), 2)
        self.x = lax.rem(self.dp, 2)

    def device(self, axis, way=0):
        if axis == "core":
            return (self.dp, 1 - self.rep)
        if axis == "x":
            return (self.dp + 1 - 2 * self.x, self.rep)
        if axis == "y":
            return (self.dp + 2 - 4 * self.y, self.rep)
        return (self.dp + 4 * (self.along(way) - self.z), self.rep)

    def along(self, way):
        return lax.rem(self.z + way + self.length, self.length)

    def greet(self):
        barrier = pltpu.get_barrier_semaphore()
        peers = [("core", 0), ("x", 0), ("y", 0)] + [("z", way) for way in range(1, self.length)]
        for axis, way in peers:
            pl.semaphore_signal(barrier, inc=1, device_id=self.device(axis, way), device_id_type=MESH)
        pl.semaphore_wait(barrier, len(peers))


class Move:
    def __init__(self, send, recv, slot, device, source, target, landing):
        self.out = pltpu.make_async_remote_copy(
            src_ref=source, dst_ref=target, send_sem=send.at[slot], recv_sem=recv.at[slot],
            device_id=device, device_id_type=MESH)
        self.into = pltpu.make_async_remote_copy(
            src_ref=landing, dst_ref=landing, send_sem=send.at[slot], recv_sem=recv.at[slot],
            device_id=device, device_id_type=MESH)

    def start(self):
        self.out.start()

    def wait(self):
        self.into.wait_recv()

    def drain(self):
        self.out.wait_send()


class Slots:
    def __init__(self, send, recv):
        self.send, self.recv, self.made = send, recv, []

    def move(self, *args):
        self.made.append(Move(self.send, self.recv, len(self.made), *args))
        return self.made[-1]

    def drain(self):
        for move in self.made:
            move.drain()


class Locals:
    def __init__(self, semaphores):
        self.semaphores, self.made = semaphores, []

    def copy(self, source, target):
        self.made.append(pltpu.make_async_copy(source, target, self.semaphores.at[len(self.made)]))
        self.made[-1].start()
        return self.made[-1]


class Gather:
    def __init__(self, links, slots, view, order, halved):
        z, y, x, length = links.z, links.y, links.x, links.length
        here = {"z": z, "y": y, "x": x}
        mine = view(z, y, x)
        self.moves = [[
            slots.move(links.device("z", way), mine, mine, view(links.along(-way), y, x))
            for way in range(1, length)]]
        here["z"] = ALL
        for axis in order:
            mine = view(here["z"], here["y"], here["x"])
            other = dict(here)
            other[axis] = 1 - here[axis]
            self.moves.append([
                slots.move(links.device(axis), mine, mine, view(other["z"], other["y"], other["x"]))])
            here[axis] = ALL
        if halved:
            mine = view(ALL, ALL, ALL)
            self.moves.append([
                slots.move(links.device("core"), mine, mine, view(ALL, ALL, ALL, 1 - links.rep))])

    def step(self, number):
        if 0 < number <= len(self.moves):
            for move in self.moves[number - 1]:
                move.wait()
        if 0 <= number < len(self.moves):
            for move in self.moves[number]:
                move.start()


class Reduce:
    def __init__(self, links, slots, own, order, lands_b, lands_a, lands_z, finish):
        self.own, self.links, self.finish, self.lands_z = own, links, finish, lands_z
        self.moves, self.adds = [], []
        z, y, x, length = links.z, links.y, links.x, links.length
        here = {"z": ALL, "y": ALL, "x": ALL}
        for axis, lands in zip(order, (lands_b, lands_a)):
            away, home = dict(here), dict(here)
            place = {"y": y, "x": x}[axis]
            away[axis], home[axis] = 1 - place, place
            self.moves.append([slots.move(
                links.device(axis), own(away["z"], away["y"], away["x"]), lands, lands)])
            here = home
            self.adds.append(functools.partial(add_into, own(home["z"], home["y"], home["x"]), lands))
        self.moves.append([
            slots.move(links.device("z", way), own(links.along(way), y, x), lands_z.at[way - 1], lands_z.at[way - 1])
            for way in range(1, length)])
        self.adds.append(self.end)

    def step(self, number):
        if 0 < number <= len(self.moves):
            for move in self.moves[number - 1]:
                move.wait()
            self.adds[number - 1]()
        if 0 <= number < len(self.moves):
            for move in self.moves[number]:
                move.start()

    def end(self):
        links = self.links
        total = self.own(links.z, links.y, links.x)[...].astype(F32)
        for way in range(1, links.length):
            total = total + self.lands_z[way - 1].astype(F32)
        self.finish(total)


def add_into(target, arrived):
    lead = target.shape[:-2]
    count = 1
    for size in lead:
        count *= size

    @pl.loop(0, count)
    def _(flat):
        index = []
        for size in reversed(lead):
            index.insert(0, lax.rem(flat, size))
            flat = lax.div(flat, size)
        index = tuple(index)
        target[index] = (target[index].astype(F32) + arrived[index].astype(F32)).astype(target.dtype)


def run(items, depth, tick):
    for number, item in enumerate(items):
        if 0 <= tick - number < depth:
            for part in item:
                part.step(tick - number)


def matmul(left, right):
    return jnp.dot(left, right, preferred_element_type=F32)


def matmul_left(left, right):
    return lax.dot_general(left, right, (((0,), (0,)), ((), ())), preferred_element_type=F32)


def matmul_right(left, right):
    return lax.dot_general(left, right, (((1,), (1,)), ((), ())), preferred_element_type=F32)


def layer_norm(values, gain, offset):
    centre = jnp.mean(values, axis=-1, keepdims=True)
    shifted = values - centre
    spread = jnp.mean(shifted * shifted, axis=-1, keepdims=True)
    return shifted * lax.rsqrt(spread + epsilon) * gain + offset


def layer_norm_back(values, gain, upstream):
    centre = jnp.mean(values, axis=-1, keepdims=True)
    shifted = values - centre
    spread = jnp.mean(shifted * shifted, axis=-1, keepdims=True)
    rate = lax.rsqrt(spread + epsilon)
    normed = shifted * rate
    scaled = upstream * gain
    first = jnp.mean(scaled, axis=-1, keepdims=True)
    second = jnp.mean(scaled * normed, axis=-1, keepdims=True)
    return rate * (scaled - first - normed * second), upstream * normed


def gelu_exact(values):
    return 0.5 * values * (1.0 + jax.scipy.special.erf(values * 0.7071067811865476))


def gelu_parts(values):
    cumulative = 0.5 * (1.0 + lax.erf(values * 0.7071067811865476))
    density = 0.3989422804014327 * jnp.exp(-0.5 * values * values)
    return values * cumulative, cumulative + values * density


def tiles(count, size, action):
    @pl.loop(0, count)
    def _(number):
        action(pl.multiple_of(number * size, size))


def head_mask(rows, columns):
    heads = columns // HEAD_DIM
    row = lax.broadcasted_iota(jnp.int32, (rows * heads, columns), 0)
    column = lax.broadcasted_iota(jnp.int32, (rows * heads, columns), 1)
    head_row = jnp.zeros_like(row)
    head_column = jnp.zeros_like(row)
    for head in range(1, heads):
        head_row = head_row + jnp.where(row >= head * rows, 1, 0)
        head_column = head_column + jnp.where(column >= head * HEAD_DIM, 1, 0)
    return jnp.where(head_row == head_column, 1.0, 0.0)


def spread_heads(rows, mask):
    return jnp.concatenate([rows] * (mask.shape[0] // rows.shape[0]), axis=0) * mask


def pick_heads(stacked, mask, rows):
    kept = stacked * mask
    total = kept[:rows]
    for head in range(1, stacked.shape[0] // rows):
        total = total + kept[head * rows:(head + 1) * rows]
    return total


def softmax(scores):
    exponent = jnp.exp(scores - jnp.max(scores, axis=-1, keepdims=True))
    return exponent / jnp.sum(exponent, axis=-1, keepdims=True)


class VectorSum:
    def __init__(self, links, slots, total, stage, lands):
        self.total, self.stage, self.lands, self.length = total, stage, lands, links.length
        self.moves = [[slots.move(links.device(axis), stage.at[number], lands.at[number], lands.at[number])]
                      for number, axis in enumerate(("core", "x", "y"))]
        self.moves.append([
            slots.move(links.device("z", way), stage.at[3], lands.at[2 + way], lands.at[2 + way])
            for way in range(1, links.length)])

    def step(self, number):
        if 0 < number <= 4:
            for move in self.moves[number - 1]:
                move.wait()
            for land in ([number - 1] if number < 4 else range(3, 2 + self.length)):
                self.total[...] = self.total[...] + self.lands[land]
        if number < 4:
            self.stage[number] = self.total[...]
            for move in self.moves[number]:
                move.start()


def layer_kernel(length, scaling, counts, media, latents, grad_out, packed, query_shard, context_shard,
                 output_shard, up_shard, down_shard, latents_out, media_grad_out, latents_grad_out, sums_out, grads_out,
                 query_all, context_all, output_all, up_all, down_all,
                 packed_all, vectors, media_in, latents_in, grad_in, context, key_value, query, attended, after,
                 feed, feed_t, branch, branch_t, pool, active, after_feed, d_feed, after_lands,
                 d_feed_lands, out_stage, grad_up, grad_down, mask, sums, total, total_stage, total_lands,
                 lands_b, lands_a, lands_z, result, send, recv, local):
    links = Links(length)
    z, y, x, rep = links.z, links.y, links.x, links.rep
    slots, locals_ = Slots(send, recv), Locals(local)
    slot_count, patches, width = media.shape
    latent_count = latents.shape[1]
    key_count = patches + latent_count
    rows = slot_count * latent_count
    both = 2 * rows
    inner = query.shape[-1]
    chunk = pool.shape[-1]
    chunks = length
    xy, yx = ("x", "y"), ("y", "x")

    staged = [locals_.copy(packed, packed_all.at[z, y, x])]
    for shard, whole in ((context_shard, context_all), (query_shard, query_all), (output_shard, output_all)):
        half = whole.shape[-2]
        staged.append(locals_.copy(shard.at[pl.ds(pl.multiple_of(rep * half, 16), half)], whole.at[z, y, x, rep]))
    grad_load = locals_.copy(grad_out, grad_in)
    half = down_all.shape[-2]
    staged.append(locals_.copy(down_shard.at[pl.ds(pl.multiple_of(rep * half, 16), half)], down_all.at[z, y, x]))
    for block in range(up_all.shape[-1] // half):
        begin = pl.multiple_of((2 * block + rep) * half, half)
        staged.append(locals_.copy(
            up_shard.at[:, pl.ds(begin, half)], up_all.at[z, y, x, :, pl.ds(block * half, half)]))
    latents_load = locals_.copy(latents, latents_in)
    media_load = locals_.copy(media, media_in)
    links.greet()
    for copy in staged:
        copy.wait()

    def halves(whole, begin, size, order):
        def view(zi, yi, xi, half=rep):
            return whole.at[zi, yi, xi, half, :, pl.ds(begin, size)]

        return Gather(links, slots, view, order, True)

    def columns(whole, begin, size, order):
        return Gather(links, slots, lambda zi, yi, xi: whole.at[zi, yi, xi, :, pl.ds(begin, size)], order, False)

    gathers = [
        [Gather(links, slots, lambda zi, yi, xi: packed_all.at[zi, yi, xi], xy, False),
         halves(context_all, 0, width // 2, xy), halves(context_all, width // 2, width // 2, yx)],
        [halves(query_all, 0, inner, xy), halves(output_all, 0, width, yx)],
    ]
    for whole in (down_all, up_all):
        part = whole.shape[-1] // (2 * chunks)
        for number in range(chunks):
            gathers.append(
                [columns(whole, 2 * number * part, part, xy), columns(whole, (2 * number + 1) * part, part, yx)])
    gathered = len(slots.made)

    def pump(tick):
        run(gathers, 5, tick)

    pump(0)
    grad_load.wait()
    count = counts[0]

    def keep(j):
        return jnp.where(j < count, 1.0, 0.0)

    for j in range(slot_count):
        branch[pl.ds(j * latent_count, latent_count)] = (grad_in[j].astype(F32) * keep(j)).astype(BF16)
    branch_move = slots.move(links.device("core"), branch.at[pl.ds(0, rows)], branch.at[pl.ds(rows, rows)],
                             branch.at[pl.ds(rows, rows)])
    branch_move.start()
    mask[...] = head_mask(latent_count, GROUP)
    sums[...] = jnp.zeros_like(sums)
    pump(1)
    latents_load.wait()
    media_load.wait()
    pump(2)
    pump(3)
    lane = packed_all.shape[-1]
    for zi in range(length):
        for yi in range(2):
            place = (zi * 2 + yi) * lane
            vectors[:, place:place + lane] = (packed_all[zi, yi, 0] + packed_all[zi, yi, 1]).astype(F32)[:8]

    step = 32

    def normalise_slot(j):
        def media_tile(at):
            context[j, pl.ds(at, step)] = layer_norm(
                media_in[j, pl.ds(at, step)].astype(F32), vectors[0:1], vectors[1:2]).astype(BF16)

        def latent_tile(at):
            context[j, pl.ds(patches + at, step)] = layer_norm(
                latents_in[j, pl.ds(at, step)].astype(F32), vectors[2:3], vectors[3:4]).astype(BF16)

        tiles(patches // step, step, media_tile)
        tiles(latent_count // step, step, latent_tile)

    pl.loop(0, slot_count)(normalise_slot)
    pump(4)

    weight_step = 256

    def key_value_slot(j):
        def body(at):
            weight = context_all[:, :, :, :, :, pl.ds(at, weight_step)].reshape(width, weight_step)
            key_value[j, :, pl.ds(at, weight_step)] = matmul(context[j], weight).astype(BF16)

        tiles(width // weight_step, weight_step, body)

    pl.loop(0, slot_count)(key_value_slot)
    pump(5)

    latent_normed = context[:, patches:, :].reshape(rows, width)
    query[...] = (matmul(latent_normed, query_all[...].reshape(width, inner)) * scaling).astype(BF16).reshape(
        slot_count, latent_count, inner)

    def attention_slot(j):
        for begin in range(0, inner, GROUP):
            stacked = spread_heads(query[j, :, begin:begin + GROUP], mask[...].astype(BF16))
            probs = softmax(matmul_right(stacked, key_value[j, :, begin:begin + GROUP])).astype(BF16)
            value = matmul(probs, key_value[j, :, inner + begin:inner + begin + GROUP])
            attended[j, :, begin:begin + GROUP] = pick_heads(value, mask[...], latent_count).astype(BF16)

    pl.loop(0, slot_count)(attention_slot)
    pump(6)

    def output_tile(at):
        weight = output_all[:, :, :, :, :, pl.ds(at, weight_step)].reshape(inner, weight_step)
        after[:, pl.ds(at, weight_step)] = latents_in[:, :, pl.ds(at, weight_step)].reshape(
            rows, weight_step).astype(F32) + matmul(attended[...].reshape(rows, inner), weight)

    tiles(width // weight_step, weight_step, output_tile)

    def feed_tile(at):
        feed[pl.ds(at, step)] = layer_norm(after[pl.ds(at, step)], vectors[4:5], vectors[5:6]).astype(BF16)

    tiles(rows // step, step, feed_tile)
    feed_move = slots.move(links.device("core"), feed.at[pl.ds(0, rows)], feed.at[pl.ds(rows, rows)],
                           feed.at[pl.ds(rows, rows)])
    feed_move.start()
    pump(7)
    branch_move.wait()

    def turn(source, target):
        def body(at):
            target[pl.ds(at, weight_step)] = source[:, pl.ds(at, weight_step)].T

        tiles(width // weight_step, weight_step, body)

    turn(branch, branch_t)
    feed_move.wait()
    turn(feed, feed_t)
    pump(8)
    tall = rows
    short = 128

    def reduction(own, lands, windows, order, keep_total):
        return Reduce(links, slots, own, order, lands[0].at[(ALL, ALL) + windows], lands[1].at[(ALL,) + windows],
                      lands[2].at[(ALL,) + windows], keep_total)

    def halved_reduction(own, lands, target, height, begin, size, along_rows):
        made = []
        for which, order in enumerate((yx, xy)):
            window = pl.ds(begin + which * size, size)
            windows = (window, pl.ds(0, target.shape[1])) if along_rows else (pl.ds(0, height), window)

            def finish(value, windows=windows):
                target[windows] = value

            made.append(reduction(lambda zi, yi, xi, windows=windows: own(zi, yi, xi, *windows), lands, windows, order, finish))
        return made

    up_lands, down_lands, query_lands, context_lands, output_lands = zip(lands_b, lands_a, lands_z)
    up_result, down_result, query_result, context_result, output_result = result
    reductions = []

    def send_off(tick):
        run(reductions, 4, tick)

    for c in range(chunks):
        def d_active_tile(at, c=c):
            weight = down_all[c].reshape(chunk, width)
            pool[pl.ds(c * both + at, tall)] = matmul_right(branch[pl.ds(at, tall)], weight).astype(BF16)

        tiles(both // tall, tall, d_active_tile)
    d_hidden = pool.at[pl.ds(chunks * both, both)]
    for c in range(chunks):
        pump(9 + c)
        begin = c * chunk

        def hidden_tile(at, c=c, begin=begin):
            weight = up_all[:, :, :, :, begin:begin + chunk].reshape(width, chunk)
            value, slope = gelu_parts(matmul(feed[pl.ds(at, short)], weight))
            active[pl.ds(at, short)] = value.astype(BF16)
            d_hidden[pl.ds(at, short)] = (pool[pl.ds(c * both + at, short)].astype(F32) * slope).astype(BF16)

        tiles(both // short, short, hidden_tile)

        def forward_tile(at, c=c):
            value = matmul(active[pl.ds(at, tall)], down_all[c].reshape(chunk, width))
            after_feed[pl.ds(at, tall)] = value if c == 0 else after_feed[pl.ds(at, tall)] + value

        def back_tile(at, c=c, begin=begin):
            weight = up_all[:, :, :, :, begin:begin + chunk].reshape(width, chunk)
            value = matmul_right(d_hidden[pl.ds(at, tall)], weight)
            d_feed[pl.ds(at, tall)] = value if c == 0 else d_feed[pl.ds(at, tall)] + value

        tiles(both // tall, tall, forward_tile)
        tiles(both // tall, tall, back_tile)
        if c == chunks - 1:
            for move in slots.made[:gathered]:
                move.drain()
            d_feed_move = slots.move(links.device("core"), d_feed.at[pl.ds(rows, rows)], d_feed_lands, d_feed_lands)
            after_move = slots.move(links.device("core"), after_feed.at[pl.ds(rows, rows)], after_lands, after_lands)
            d_feed_move.start()
            after_move.start()

        def grad_tile(zi, begin=begin, c=c):
            place = pl.multiple_of(zi * (width // length), width // length)
            up = matmul(feed_t[pl.ds(place, width // length)], d_hidden[...]).astype(BF16)
            grad_up[zi, :, :, :, begin:begin + chunk] = up.reshape(2, 2, width // (4 * length), chunk)
            down = matmul(branch_t[pl.ds(place, width // length)], active[...]).astype(BF16)
            block = chunk // 4
            for number in range(4):
                grad_down[c, number // 2, number % 2, pl.ds(place, width // length)] = down[
                    :, number * block:(number + 1) * block]

        pl.loop(0, length)(grad_tile)
        reductions.append(halved_reduction(
            lambda zi, yi, xi, *w: grad_up.at[(zi, yi, xi) + w], up_lands, up_result, up_result.shape[0],
            begin, chunk // 2, False))
        send_off(c)
    part = width // chunks
    for number in range(chunks):
        reductions.append(halved_reduction(
            lambda zi, yi, xi, *w: grad_down.at[(zi, yi, xi) + w], down_lands, down_result, width,
            number * part, part // 2, True))

    d_feed_move.wait()
    feed_move.drain()

    def fold(terms):
        return jnp.sum(terms.reshape(-1, 8, width), axis=0)

    def middle_slot(j):
        def body(at):
            own = pl.ds(pl.multiple_of(j * latent_count + at, step), step)
            upstream = d_feed[own] + d_feed_lands[own]
            d_norm, gain_terms = layer_norm_back(after[own], vectors[4:5], upstream)
            sums[4] = sums[4] + fold(gain_terms)
            sums[5] = sums[5] + fold(upstream)
            d_middle = grad_in[j, pl.ds(at, step)].astype(F32) * keep(j) + d_norm
            d_feed[own] = d_middle
            feed[own] = d_middle.astype(BF16)

        tiles(latent_count // step, step, body)

    pl.loop(0, slot_count)(middle_slot)
    send_off(4)
    after_move.wait()
    for j in range(slot_count):
        own = pl.ds(j * latent_count, latent_count)
        out_stage[j] = ((after[own] + after_feed[own] + after_lands[own]) * keep(j)).astype(BF16)
    written = [locals_.copy(out_stage, latents_out)]

    output_rows, context_rows = output_all.shape[-2], context_all.shape[-2]
    output_at = 3 * down_all.shape[-2] // 4

    def output_own(zi, yi, xi, half, *w):
        return down_all.at[zi, yi, xi, pl.ds(pl.multiple_of(output_at + half * output_rows, 16), output_rows), w[1]]

    def context_own(zi, yi, xi, half, *w):
        return up_all.at[zi, yi, xi, pl.ds(pl.multiple_of(half * context_rows, 16), context_rows), w[1]]

    def query_own(zi, yi, xi, half, *w):
        moved = pl.ds(2 * inner + w[1].start, w[1].size)
        return up_all.at[zi, yi, xi, pl.ds(pl.multiple_of(half * context_rows, 16), context_rows), moved]

    sibling_lands = {
        "context": down_all.at[:, :, :, pl.ds(0, context_rows)],
        "query": down_all.at[:, :, :, pl.ds(context_rows, context_rows), pl.ds(0, inner)],
        "output": down_all.at[:, :, :, pl.ds(2 * context_rows, output_rows)],
    }

    def to_sibling(own, name, size):
        whole = (None, pl.ds(0, size))
        move = slots.move(links.device("core"), own(ALL, ALL, ALL, 1 - rep, *whole), sibling_lands[name],
                          sibling_lands[name])
        move.start()

        def settle():
            move.wait()
            add_into(own(ALL, ALL, ALL, rep, *whole), sibling_lands[name])

        return settle

    d_branch = feed.at[pl.ds(0, rows)]
    output_block = inner // length

    def output_grad_tile(zi):
        place = pl.multiple_of(zi * output_block, output_block)
        turned = attended[:, :, pl.ds(place, output_block)].reshape(rows, output_block).T
        value = matmul(turned, d_branch[...]).astype(BF16)
        down_all[zi, :, :, output_at:] = value.reshape(2, 2, output_block // 4, width)

    pl.loop(0, length)(output_grad_tile)
    settle_output = to_sibling(output_own, "output", width)
    d_attended, d_query = active.at[pl.ds(0, rows)], active.at[pl.ds(rows, rows)]
    d_attended[...] = matmul_right(d_branch[...], output_all[...].reshape(inner, width)).astype(BF16)
    send_off(5)

    def attention_back_slot(j):
        own = pl.ds(pl.multiple_of(j * latent_count, latent_count), latent_count)
        for begin in range(0, inner, GROUP):
            keys = key_value[j, :, begin:begin + GROUP]
            values = key_value[j, :, inner + begin:inner + begin + GROUP]
            low_mask = mask[...].astype(BF16)
            stacked = spread_heads(query[j, :, begin:begin + GROUP], low_mask)
            upstream = spread_heads(d_attended[own, begin:begin + GROUP], low_mask)
            probs = softmax(matmul_right(stacked, keys))
            d_probs = matmul_right(upstream, values)
            d_scores = (probs * (d_probs - jnp.sum(probs * d_probs, axis=-1, keepdims=True))).astype(BF16)
            d_query[own, begin:begin + GROUP] = (
                pick_heads(matmul(d_scores, keys), mask[...], latent_count).astype(BF16).astype(F32) * scaling
            ).astype(BF16)
            at = pl.multiple_of(j * 2 * key_count, 16)
            pool[pl.ds(at, key_count), begin:begin + GROUP] = matmul_left(d_scores, stacked).astype(BF16)
            pool[pl.ds(at + key_count, key_count), begin:begin + GROUP] = matmul_left(
                probs.astype(BF16), upstream).astype(BF16)

    pl.loop(0, 2)(attention_back_slot)
    send_off(6)
    pl.loop(2, slot_count)(attention_back_slot)
    send_off(7)

    block = width // length

    def query_grad_tile(zi):
        place = pl.multiple_of(zi * block, block)
        turned = context[:, patches:, pl.ds(place, block)].reshape(rows, block).T
        value = matmul(turned, d_query[...]).astype(BF16)
        up_all[zi, :, :, :, 2 * inner:3 * inner] = value.reshape(2, 2, block // 4, inner)

    pl.loop(0, length)(query_grad_tile)
    settle_query = to_sibling(query_own, "query", inner)

    def context_grad_tile(zi):
        place = pl.multiple_of(zi * block, block)
        for which in range(2):
            value = None
            for j in range(slot_count):
                turned = context[j, :, pl.ds(place, block)].T
                at = (2 * j + which) * key_count
                term = matmul(turned, pool[at:at + key_count])
                value = term if value is None else value + term
            up_all[zi, :, :, :, which * inner:(which + 1) * inner] = value.astype(BF16).reshape(
                2, 2, block // 4, inner)

    pl.loop(0, length)(context_grad_tile)
    settle_context = to_sibling(context_own, "context", width)
    settle_output()
    settle_query()
    reductions.append(
        halved_reduction(lambda zi, yi, xi, *w: output_own(zi, yi, xi, rep, *w), output_lands, output_result,
                         output_rows, 0, width // 2, False)
        + halved_reduction(lambda zi, yi, xi, *w: query_own(zi, yi, xi, rep, *w), query_lands, query_result,
                           context_rows, 0, inner // 2, False))
    send_off(8)
    settle_context()
    reductions.append(halved_reduction(
        lambda zi, yi, xi, *w: context_own(zi, yi, xi, rep, *w), context_lands, context_result, context_rows,
        0, width // 2, False))
    send_off(9)

    upstream_rows = d_feed_lands

    def input_slot(j):
        at = pl.multiple_of(j * 2 * key_count, 16)

        def upstream_tile(number):
            weight = context_all[number].reshape(block, 2 * inner)
            place = pl.ds(pl.multiple_of(number * block, block), block)
            upstream_rows[:, place] = (matmul_right(pool[pl.ds(at, key_count)], weight[:, :inner])
                                       + matmul_right(pool[pl.ds(at + key_count, key_count)], weight[:, inner:]))
            own = pl.ds(pl.multiple_of(j * latent_count, latent_count), latent_count)
            upstream_rows[patches:, place] = upstream_rows[patches:, place] + matmul_right(
                d_query[own], query_all[number].reshape(block, inner))

        pl.loop(0, length)(upstream_tile)

        def media_tile(at):
            own = pl.ds(at, step)
            upstream = upstream_rows[own]
            value, gain_terms = layer_norm_back(media_in[j, own].astype(F32), vectors[0:1], upstream)
            sums[0] = sums[0] + fold(gain_terms)
            sums[1] = sums[1] + fold(upstream)
            media_in[j, own] = value.astype(BF16)

        def latent_tile(at):
            own = pl.ds(at, step)
            upstream = upstream_rows[pl.ds(patches + at, step)]
            value, gain_terms = layer_norm_back(latents_in[j, own].astype(F32), vectors[2:3], upstream)
            sums[2] = sums[2] + fold(gain_terms)
            sums[3] = sums[3] + fold(upstream)
            d_middle = d_feed[pl.ds(pl.multiple_of(j * latent_count + at, step), step)]
            latents_in[j, own] = (d_middle + value).astype(BF16)

        tiles(patches // step, step, media_tile)
        tiles(latent_count // step, step, latent_tile)

    pl.loop(0, 2)(input_slot)
    send_off(10)
    pl.loop(2, slot_count)(input_slot)
    written.append(locals_.copy(media_in, media_grad_out))
    written.append(locals_.copy(latents_in, latents_grad_out))
    total[...] = jnp.zeros_like(total)
    for number in range(6):
        total[number:number + 1] = jnp.sum(sums[number], axis=0, keepdims=True)
    vector_sum = VectorSum(links, slots, total, total_stage, total_lands)
    vector_sum.step(0)
    send_off(11)
    vector_sum.step(1)
    send_off(12)
    for number in range(2, 5):
        vector_sum.step(number)
    sums_out[...] = total[...]
    for value, out in zip(result, grads_out):
        written.append(locals_.copy(value, out.at[rep]))
        move = slots.move(links.device("core"), value, out.at[rep], out.at[1 - rep])
        move.start()
        written.append(move)
    for copy in written:
        copy.wait()
    drained = slots.made[gathered:]
    for move in drained:
        if move is not feed_move:
            move.drain()


def layer(length, counts, media, latents, grad_out, packed, shards):
    query_shard, context_shard, output_shard, up_shard, down_shard = shards
    slot_count, patches, width = media.shape
    latent_count = latents.shape[1]
    key_count = patches + latent_count
    rows = slot_count * latent_count
    inner = query_shard.shape[1]
    hidden = up_shard.shape[1] // 2
    chunk = hidden // length
    blocks = (length, 2, 2)

    def halved(shard):
        return blocks + (2, shard.shape[0] // 2, shard.shape[1])

    grad_up_shape = blocks + (up_shard.shape[0], hidden)
    grad_down_shape = blocks + (width, down_shard.shape[0] // 2)
    results = [grad_up_shape[3:], grad_down_shape[3:]] + [halved(s)[4:] for s in shards[:3]]
    anywhere = pl.BlockSpec(memory_space=pl.ANY)
    vmem = pl.BlockSpec(memory_space=pltpu.VMEM)
    sums_shape = (8, width)
    scratch = [
        pltpu.VMEM(halved(query_shard), BF16),
        pltpu.VMEM(halved(context_shard), BF16),
        pltpu.VMEM(halved(output_shard), BF16),
        pltpu.VMEM(grad_up_shape, BF16),
        pltpu.VMEM(blocks + (down_shard.shape[0] // 2, width), BF16),
        pltpu.VMEM(blocks + packed.shape, BF16),
        pltpu.VMEM((8, width), F32),
        pltpu.VMEM(media.shape, BF16),
        pltpu.VMEM(latents.shape, BF16),
        pltpu.VMEM(grad_out.shape, BF16),
        pltpu.VMEM((slot_count, key_count, width), BF16),
        pltpu.VMEM((slot_count, key_count, 2 * inner), BF16),
        pltpu.VMEM((slot_count, latent_count, inner), BF16),
        pltpu.VMEM((slot_count, latent_count, inner), BF16),
        pltpu.VMEM((rows, width), F32),
        pltpu.VMEM((2 * rows, width), BF16),
        pltpu.VMEM((width, 2 * rows), BF16),
        pltpu.VMEM((2 * rows, width), BF16),
        pltpu.VMEM((width, 2 * rows), BF16),
        pltpu.VMEM((max((length + 1) * 2 * rows, 2 * slot_count * key_count), chunk), BF16),
        pltpu.VMEM((2 * rows, chunk), BF16),
        pltpu.VMEM((2 * rows, width), F32),
        pltpu.VMEM((2 * rows, width), F32),
        pltpu.VMEM((rows, width), F32),
        pltpu.VMEM((rows, width), F32),
        pltpu.VMEM(latents.shape, BF16),
        pltpu.VMEM(grad_up_shape, BF16),
        pltpu.VMEM(grad_down_shape, BF16),
        pltpu.VMEM((latent_count * (GROUP // HEAD_DIM), GROUP), F32),
        pltpu.VMEM((6, 8, width), F32),
        pltpu.VMEM(sums_shape, F32),
        pltpu.VMEM((4,) + sums_shape, F32),
        pltpu.VMEM((2 + length,) + sums_shape, F32),
        [pltpu.VMEM((length, 2) + r, BF16) for r in results],
        [pltpu.VMEM((length,) + r, BF16) for r in results],
        [pltpu.VMEM((length - 1,) + r, BF16) for r in results],
        [pltpu.VMEM(r, F32) for r in results],
        pltpu.SemaphoreType.DMA((240,)),
        pltpu.SemaphoreType.DMA((240,)),
        pltpu.SemaphoreType.DMA((64,)),
    ]
    out_shape = (
        jax.ShapeDtypeStruct(latents.shape, BF16), jax.ShapeDtypeStruct(media.shape, BF16),
        jax.ShapeDtypeStruct(latents.shape, BF16), jax.ShapeDtypeStruct(sums_shape, F32),
        [jax.ShapeDtypeStruct((2,) + r, F32) for r in results])
    return pl.pallas_call(
        functools.partial(layer_kernel, length, HEAD_DIM ** (-0.5)),
        out_shape=out_shape,
        in_specs=[pl.BlockSpec(memory_space=pltpu.SMEM)] + [anywhere] * 9,
        out_specs=(anywhere, anywhere, anywhere, vmem, [anywhere] * 5),
        scratch_shapes=scratch,
        compiler_params=pltpu.CompilerParams(
            collective_id=0, has_side_effects=True, vmem_limit_bytes=63 * 2 ** 20),
        name="resampler_layer",
    )(counts, media, latents, grad_out, packed, query_shard, context_shard, output_shard, up_shard, down_shard)


def head_scores(first_heads, second_heads):
    return jnp.einsum(
        "bqhd,bkhd->bhqk", first_heads, second_heads, preferred_element_type=jnp.float32
    )


def collective_body(
    media,
    latents,
    image_counts,
    grad_out,
    media_gain,
    media_bias,
    latent_gain,
    latent_bias,
    feed_gain,
    feed_bias,
    query_weight,
    context_weight,
    output_weight,
    up_weight,
    down_weight,
):
    samples, slots, patches, model_width = media.shape
    latent_count = latents.shape[2]
    inner_width = query_weight.shape[1]
    head_count = inner_width // HEAD_DIM
    blocks = samples * slots
    key_count = patches + latent_count
    latent_total = blocks * latent_count
    scaling = HEAD_DIM ** (-0.5)
    vector_shards = (media_gain, media_bias, latent_gain, latent_bias, feed_gain, feed_bias)
    weight_shards = (query_weight, context_weight, output_weight, up_weight, down_weight)
    gathered = tuple(lax.all_gather(s, "dp", axis=0, tiled=True) for s in vector_shards + weight_shards)
    vectors = [element.astype(jnp.float32) for element in gathered[:6]]
    media_rows = media.reshape(blocks * patches, model_width).astype(jnp.float32)
    latent_rows = latents.reshape(latent_total, model_width).astype(jnp.float32)
    media_normed = layer_norm(media_rows, vectors[0], vectors[1]).astype(jnp.bfloat16)
    latent_normed = layer_norm(latent_rows, vectors[2], vectors[3]).astype(jnp.bfloat16)
    queries = (matmul(latent_normed, gathered[6]) * scaling).astype(jnp.bfloat16)
    context = jnp.concatenate(
        [
            media_normed.reshape(blocks, patches, model_width),
            latent_normed.reshape(blocks, latent_count, model_width),
        ],
        axis=1,
    ).reshape(blocks * key_count, model_width)
    key_value = (
        matmul(context, gathered[7])
        .astype(jnp.bfloat16)
        .reshape(blocks, key_count, 2 * inner_width)
    )
    query_heads = queries.reshape(blocks, latent_count, head_count, HEAD_DIM)
    key_heads = key_value[:, :, :inner_width].reshape(blocks, key_count, head_count, HEAD_DIM)
    value_heads = key_value[:, :, inner_width:].reshape(blocks, key_count, head_count, HEAD_DIM)
    scores = head_scores(query_heads, key_heads)
    row_max = jnp.max(scores, axis=-1, keepdims=True)
    exponent = jnp.exp(scores - row_max)
    row_total = jnp.sum(exponent, axis=-1, keepdims=True)
    log_total = row_max + jnp.log(row_total)
    attention_weights = (exponent / row_total).astype(jnp.bfloat16)
    attended = (
        jnp.einsum(
            "bhqk,bkhd->bqhd", attention_weights, value_heads, preferred_element_type=jnp.float32
        )
        .astype(jnp.bfloat16)
        .reshape(latent_total, inner_width)
    )
    after_attention = latent_rows + matmul(attended, gathered[8])
    feed_input = layer_norm(after_attention, vectors[4], vectors[5]).astype(jnp.bfloat16)
    hidden = matmul(feed_input, gathered[9])
    activated = gelu_exact(hidden).astype(jnp.bfloat16)
    after_feed = after_attention + matmul(activated, gathered[10])
    slot_mask = (
        lax.broadcasted_iota(jnp.int32, (samples, slots), 1) < image_counts[:, None]
    ).astype(jnp.float32)
    row_mask = jnp.broadcast_to(slot_mask[:, :, None], (samples, slots, latent_count)).reshape(
        latent_total, 1
    )
    latents_out = (after_feed * row_mask).astype(jnp.bfloat16).reshape(latents.shape)
    backward_set = gathered
    back_vectors = [element.astype(jnp.float32) for element in backward_set[:6]]
    d_after = grad_out.reshape(latent_total, model_width).astype(jnp.float32) * row_mask
    d_branch = d_after.astype(jnp.bfloat16)
    grad_down = matmul_left(activated, d_branch)
    d_activated = matmul_right(d_branch, backward_set[10])
    d_hidden = jax.vjp(gelu_exact, hidden)[1](d_activated)[0].astype(jnp.bfloat16)
    grad_up = matmul_left(feed_input, d_hidden)
    d_feed = matmul_right(d_hidden, backward_set[9])
    d_feed_norm, grad_feed_gain, grad_feed_bias = jax.vjp(
        layer_norm, after_attention, back_vectors[4], back_vectors[5]
    )[1](d_feed)
    d_middle = d_after + d_feed_norm
    d_out_branch = d_middle.astype(jnp.bfloat16)
    grad_output = matmul_left(attended, d_out_branch)
    d_attended = (
        matmul_right(d_out_branch, backward_set[8])
        .astype(jnp.bfloat16)
        .reshape(blocks, latent_count, head_count, HEAD_DIM)
    )
    recomputed = jnp.exp(head_scores(query_heads, key_heads) - log_total)
    d_weights = head_scores(d_attended, value_heads)
    d_scores = (
        recomputed * (d_weights - jnp.sum(recomputed * d_weights, axis=-1, keepdims=True))
    ).astype(jnp.bfloat16)
    d_queries = (
        jnp.einsum(
            "bhqk,bkhd->bqhd", d_scores, key_heads, preferred_element_type=jnp.float32
        ).astype(jnp.bfloat16)
        * scaling
    ).reshape(latent_total, inner_width)
    d_keys = jnp.einsum(
        "bhqk,bqhd->bkhd", d_scores, query_heads, preferred_element_type=jnp.float32
    ).astype(jnp.bfloat16)
    d_values = jnp.einsum(
        "bhqk,bqhd->bkhd",
        recomputed.astype(jnp.bfloat16),
        d_attended,
        preferred_element_type=jnp.float32,
    ).astype(jnp.bfloat16)
    d_key_value = jnp.concatenate(
        [
            d_keys.reshape(blocks, key_count, inner_width),
            d_values.reshape(blocks, key_count, inner_width),
        ],
        axis=-1,
    ).reshape(blocks * key_count, 2 * inner_width)
    grad_query = matmul_left(latent_normed, d_queries)
    grad_context = matmul_left(context, d_key_value)
    d_context = matmul_right(d_key_value, backward_set[7]).reshape(blocks, key_count, model_width)
    d_latent_normed = matmul_right(d_queries, backward_set[6]) + d_context[:, patches:, :].reshape(
        latent_total, model_width
    )
    d_media_normed = d_context[:, :patches, :].reshape(blocks * patches, model_width)
    d_latent_norm, grad_latent_gain, grad_latent_bias = jax.vjp(
        layer_norm, latent_rows, back_vectors[2], back_vectors[3]
    )[1](d_latent_normed)
    grad_latents = (d_middle + d_latent_norm).astype(jnp.bfloat16).reshape(latents.shape)
    d_media, grad_media_gain, grad_media_bias = jax.vjp(
        layer_norm, media_rows, back_vectors[0], back_vectors[1]
    )[1](d_media_normed)
    grad_media = d_media.astype(jnp.bfloat16).reshape(media.shape)
    vector_grads = jnp.stack([
        grad_media_gain, grad_media_bias, grad_latent_gain, grad_latent_bias, grad_feed_gain, grad_feed_bias])
    weight_grads = [
        g.astype(jnp.bfloat16) for g in (grad_query, grad_context, grad_output, grad_up, grad_down)]
    vector_sums = lax.psum_scatter(vector_grads, "dp", scatter_dimension=1, tiled=True)
    summed = [lax.psum_scatter(g, "dp", scatter_dimension=0, tiled=True) for g in weight_grads]
    owned = tuple(lax.psum(vector_sums, "rep")) + tuple(
        lax.psum(s, "rep").astype(jnp.float32) for s in summed)
    return (
        latents_out,
        grad_media,
        grad_latents,
        owned[0],
        owned[1],
        owned[2],
        owned[3],
        owned[4],
        owned[5],
        owned[6],
        owned[7],
        owned[8],
        owned[9],
        owned[10],
    )


def body(media, latents, image_counts, grad_out, *parameters):
    chips = lax.axis_size("dp")
    weight_shards = parameters[6:]
    tiled = (media.shape[0] == 1 and chips % 4 == 0 and chips > 4 and parameters[0].shape[0] == 64
             and all(s.shape[0] % 32 == 0 for s in weight_shards))
    if not tiled:
        return collective_body(media, latents, image_counts, grad_out, *parameters)
    side = lax.rem(lax.axis_index("dp"), 2)
    stacked = jnp.stack(parameters[:6])
    packed = jnp.pad(
        jnp.concatenate([jnp.where(side == 0, stacked, 0), jnp.where(side == 0, 0, stacked)], axis=1), ((0, 10), (0, 0)))
    latents_out, grad_media, grad_latents, vector_sums, summed = layer(
        chips // 4, image_counts, media[0], latents[0], grad_out[0], packed, weight_shards)
    sums = [s.reshape(-1, s.shape[-1]) for s in summed[2:]]
    rows, hidden = summed[0].shape[1:]
    half = summed[1].shape[-1]
    sums.append(summed[0].reshape(2, rows, hidden // half, half).transpose(1, 2, 0, 3).reshape(rows, 2 * hidden))
    sums.append(summed[1].transpose(0, 2, 1).reshape(2 * half, -1))
    width = parameters[0].shape[0]
    mine = lax.dynamic_slice(vector_sums, (0, lax.axis_index("dp") * width), (6, width))
    return (latents_out[None], grad_media[None], grad_latents[None]) + tuple(mine) + tuple(sums)


def solution(mesh):
    return jax.shard_map(
        body,
        mesh=mesh,
        in_specs=(
            P(("dp", "rep"), None, None, None),
            P(("dp", "rep"), None, None, None),
            P(("dp", "rep")),
            P(("dp", "rep"), None, None, None),
            P("dp"),
            P("dp"),
            P("dp"),
            P("dp"),
            P("dp"),
            P("dp"),
            P("dp", None),
            P("dp", None),
            P("dp", None),
            P("dp", None),
            P("dp", None),
        ),
        out_specs=(
            P(("dp", "rep"), None, None, None),
            P(("dp", "rep"), None, None, None),
            P(("dp", "rep"), None, None, None),
            P("dp"),
            P("dp"),
            P("dp"),
            P("dp"),
            P("dp"),
            P("dp"),
            P("dp", None),
            P("dp", None),
            P("dp", None),
            P("dp", None),
            P("dp", None),
        ),
        check_vma=False,
    )
```

profile of v0, /device:TPU:0, one launch (start us, length us, event | category | flops | bytes accessed | tf_op | source)
XLA Modules:
  0.0 250.6 jit_solution(3343912902491433314)
XLA Ops:
  0.7 0.8 stack.27
  1.4 0.7 fusion.2.packed
  2.7 234.5 %resampler_layer.1 = (bf16[5,64,1024]{2,1,0:T(8,128)(2,1)}, bf16[5,256,1024]{2,1,0:T(8,128)(2,1)}, bf16[5,64,1024]{2,1,0:T(8,128)(2,1)}, f32[8,1024]{1,0:T(8,128...) custom-call(s32[1]{0:T(128)S(6)} %copy.39.counts, ...), custom_call_target="tpu_custom_call" | custom-call | tf_op jit(solution)/shard_map/resampler_layer/pallas_call | solution.py:786
  237.3 0.7 constant_dynamic-slice_fusion
  238.0 0.5 slice_bitcast_fusion
  238.6 1.4 copy.32
  240.0 0.1 bitcast_bitcast_fusion
  240.1 0.8 copy.30
  240.9 0.0 copy-start.2
  240.9 1.8 reshape.50
  242.7 0.0 copy-start
  242.7 2.7 %copy.31 = f32[2,128,1024]{2,1,0:T(8,128)} copy(f32[2,128,1024]{1,2,0:T(8,128)} %bitcast.40) | data formatting | bytes 2097152 | tf_op jit(solution)/shard_map/transpose | solution.py:983
  245.4 0.0 copy-done.2
  245.4 0.8 copy.40
  246.2 0.0 copy-done
  246.2 0.0 copy-start.1
  246.2 0.0 copy-start.5
  246.2 0.0 copy-start.3
  246.2 0.0 copy-start.4
  246.3 1.5 copy.41
  247.7 0.0 copy-done.1
  247.8 0.8 copy.42
  248.6 0.0 copy-done.5
  248.6 0.7 copy.43
  249.2 0.0 copy-done.3
  249.2 0.7 copy.44
  250.0 0.0 copy-done.4
  250.0 0.7 copy.45
  (1 shorter events, 0.0 us)
Async XLA Ops:
  240.9 4.5 %copy-start.2 = (bf16[5,64,1024]{2,1,0:T(8,128)(2,1)S(1)}, bf16[5,64,1024]{2,1,0:T(8,128)(2,1)}, u32[]{:S(2)}) copy-start(bf16[5,64,1024]{2,1,0:T(8,128)(2,1)} %get-tuple-element.23) | copy-start | bytes 1966084
  242.7 3.5 %copy-start = (bf16[5,256,1024]{2,1,0:T(8,128)(2,1)S(1)}, bf16[5,256,1024]{2,1,0:T(8,128)(2,1)}, u32[]{:S(2)}) copy-start(bf16[5,256,1024]{2,1,0:T(8,128)(2,1)} %get-tuple-element.24) | copy-start | bytes 7864324
  246.2 1.5 copy-start.1
  246.2 2.4 copy-start.5
  246.2 3.0 %copy-start.3 = (f32[2,32,1024]{2,1,0:T(8,128)S(1)}, f32[2,32,1024]{2,1,0:T(8,128)}, u32[]{:S(2)}) copy-start(f32[2,32,1024]{2,1,0:T(8,128)} %get-tuple-element.28) | copy-start | bytes 786436
  246.2 3.7 %copy-start.4 = (f32[2,16,1024]{2,1,0:T(8,128)S(1)}, f32[2,16,1024]{2,1,0:T(8,128)}, u32[]{:S(2)}) copy-start(f32[2,16,1024]{2,1,0:T(8,128)} %get-tuple-element.29) | copy-start | bytes 393220
where the time goes:
time: 251 us
  Pallas kernels  235 us (94%)
  local copies, waits for them, and re-layouts  14 us (6%)
    pallas_call x1, Pallas kernels, layer(): pl.pallas_call(functools.partial(layer_kernel, length, HEAD_DIM ** (-0.5)...  235 us
    unnamed x19, local copies, waits for them, and re-layouts  6.61 us

commit v1 on v0

--- a/solution.py
+++ b/solution.py
@@ -62,7 +62,10 @@
     def wait(self):
         self.into.wait_recv()
 
+    drained = False
+
     def drain(self):
+        self.drained = True
         self.out.wait_send()
 
 
@@ -73,10 +76,6 @@
     def move(self, *args):
         self.made.append(Move(self.send, self.recv, len(self.made), *args))
         return self.made[-1]
-
-    def drain(self):
-        for move in self.made:
-            move.drain()
 
 
 class Locals:
@@ -90,20 +89,20 @@
 
 
 class Gather:
-    def __init__(self, links, slots, view, order, halved):
-        z, y, x, length = links.z, links.y, links.x, links.length
-        here = {"z": z, "y": y, "x": x}
-        mine = view(z, y, x)
-        self.moves = [[
-            slots.move(links.device("z", way), mine, mine, view(links.along(-way), y, x))
-            for way in range(1, length)]]
-        here["z"] = ALL
-        for axis in order:
+    def __init__(self, links, slots, view, axes, halved):
+        here = {"z": links.z, "y": links.y, "x": links.x}
+        self.moves = []
+        for axis in axes:
             mine = view(here["z"], here["y"], here["x"])
-            other = dict(here)
-            other[axis] = 1 - here[axis]
-            self.moves.append([
-                slots.move(links.device(axis), mine, mine, view(other["z"], other["y"], other["x"]))])
+            if axis == "z":
+                self.moves.append([
+                    slots.move(links.device("z", way), mine, mine, view(links.along(-way), here["y"], here["x"]))
+                    for way in range(1, links.length)])
+            else:
+                other = dict(here)
+                other[axis] = 1 - here[axis]
+                self.moves.append([
+                    slots.move(links.device(axis), mine, mine, view(other["z"], other["y"], other["x"]))])
             here[axis] = ALL
         if halved:
             mine = view(ALL, ALL, ALL)
@@ -120,22 +119,24 @@
 
 
 class Reduce:
-    def __init__(self, links, slots, own, order, lands_b, lands_a, lands_z, finish):
+    def __init__(self, links, slots, own, axes, lands, lands_z, finish):
         self.own, self.links, self.finish, self.lands_z = own, links, finish, lands_z
         self.moves, self.adds = [], []
-        z, y, x, length = links.z, links.y, links.x, links.length
+        z, y, x = links.z, links.y, links.x
         here = {"z": ALL, "y": ALL, "x": ALL}
-        for axis, lands in zip(order, (lands_b, lands_a)):
+        for axis, land in zip(axes, lands):
             away, home = dict(here), dict(here)
             place = {"y": y, "x": x}[axis]
             away[axis], home[axis] = 1 - place, place
             self.moves.append([slots.move(
-                links.device(axis), own(away["z"], away["y"], away["x"]), lands, lands)])
+                links.device(axis), own(away["z"], away["y"], away["x"]), land, land)])
             here = home
-            self.adds.append(functools.partial(add_into, own(home["z"], home["y"], home["x"]), lands))
+            self.adds.append(functools.partial(add_into, own(home["z"], home["y"], home["x"]), land))
         self.moves.append([
-            slots.move(links.device("z", way), own(links.along(way), y, x), lands_z.at[way - 1], lands_z.at[way - 1])
-            for way in range(1, length)])
+            slots.move(links.device("z", way), own(links.along(way), here["y"], here["x"]), lands_z.at[way - 1],
+                       lands_z.at[way - 1])
+            for way in range(1, links.length)])
+        self.mine = own(z, here["y"], here["x"])
         self.adds.append(self.end)
 
     def step(self, number):
@@ -148,9 +149,8 @@
                 move.start()
 
     def end(self):
-        links = self.links
-        total = self.own(links.z, links.y, links.x)[...].astype(F32)
-        for way in range(1, links.length):
+        total = self.mine[...].astype(F32)
+        for way in range(1, self.links.length):
             total = total + self.lands_z[way - 1].astype(F32)
         self.finish(total)
 
@@ -171,11 +171,11 @@
         target[index] = (target[index].astype(F32) + arrived[index].astype(F32)).astype(target.dtype)
 
 
-def run(items, depth, tick):
-    for number, item in enumerate(items):
-        if 0 <= tick - number < depth:
-            for part in item:
-                part.step(tick - number)
+def run(table, tick):
+    for item, first, stride in table:
+        late = tick - first
+        if late >= 0 and late % stride == 0:
+            item.step(late // stride)
 
 
 def matmul(left, right):
@@ -275,13 +275,55 @@
                 move.start()
 
 
+class Rows:
+    def __init__(self, links, slots, buffer, count, parts):
+        self.moves, self.passed = [], []
+        for begin, size in parts:
+            def place(owner, begin=begin, size=size):
+                return buffer.at[pl.ds(owner * count + begin, size)]
+
+            self.moves.append([
+                slots.move(links.device("x"), place(0), place(2), place(2)),
+                slots.move(links.device("core"), place(0), place(1), place(1))])
+            self.passed.append(slots.move(links.device("core"), place(2), place(3), place(3)))
+
+    def send(self, part):
+        for move in self.moves[part]:
+            move.start()
+
+    def near(self, part):
+        self.moves[part][1].wait()
+
+    def forward(self, part):
+        self.moves[part][0].wait()
+        self.passed[part].start()
+
+    def far(self, part):
+        self.passed[part].wait()
+
+    def drain(self):
+        for move in [m for pair in self.moves for m in pair] + self.passed:
+            move.drain()
+
+
+class Partials:
+    def __init__(self, links, slots, stage, lands, count):
+        def place(owner):
+            return stage.at[pl.ds(owner * count, count)]
+
+        self.place, self.lands = place, lands
+        self.far = slots.move(links.device("core"), place(3), lands.at[0], lands.at[0])
+        self.near = slots.move(links.device("core"), place(1), lands.at[1], lands.at[1])
+        self.across = slots.move(links.device("x"), place(2), lands.at[2], lands.at[2])
+
+
 def layer_kernel(length, scaling, counts, media, latents, grad_out, packed, query_shard, context_shard,
                  output_shard, up_shard, down_shard, latents_out, media_grad_out, latents_grad_out, sums_out, grads_out,
-                 query_all, context_all, output_all, up_all, down_all,
+                 query_all, context_all, output_all, up_all, up_stage, down_all,
                  packed_all, vectors, media_in, latents_in, grad_in, context, key_value, query, attended, after,
-                 feed, feed_t, branch, branch_t, pool, active, after_feed, d_feed, after_lands,
-                 d_feed_lands, out_stage, grad_up, grad_down, mask, sums, total, total_stage, total_lands,
-                 lands_b, lands_a, lands_z, result, send, recv, local):
+                 feed, feed_t, branch, branch_t, pool, totals, after_lands, d_feed_lands, upstream_rows,
+                 grad_up, grad_down, grad_query, grad_output, mask, sums, total, total_stage, total_lands,
+                 own_rows_send, own_rows_land, lands_c, lands_b, lands_a, lands_z, result, send, recv, local):
     links = Links(length)
     z, y, x, rep = links.z, links.y, links.x, links.rep
     slots, locals_ = Slots(send, recv), Locals(local)
@@ -289,28 +331,30 @@
     latent_count = latents.shape[1]
     key_count = patches + latent_count
     rows = slot_count * latent_count
-    both = 2 * rows
     inner = query.shape[-1]
-    chunk = pool.shape[-1]
     chunks = length
-    xy, yx = ("x", "y"), ("y", "x")
+    hidden = up_all.shape[-1]
+    chunk = hidden // chunks
+    unit = down_all.shape[-2]
+    xy, yx = ("z", "x", "y"), ("z", "y", "x")
+
+    def unit_columns(half, number):
+        return pl.ds(pl.multiple_of(((2 * number + half) * 2 + rep) * unit, unit), unit)
 
     staged = [locals_.copy(packed, packed_all.at[z, y, x])]
     for shard, whole in ((context_shard, context_all), (query_shard, query_all), (output_shard, output_all)):
         half = whole.shape[-2]
         staged.append(locals_.copy(shard.at[pl.ds(pl.multiple_of(rep * half, 16), half)], whole.at[z, y, x, rep]))
+    later = []
+    for number in range(hidden // unit):
+        window = pl.ds(number * unit, unit)
+        later.append(locals_.copy(up_shard.at[:, unit_columns(1 - x, number)], up_stage.at[:, window]))
+        later.append(locals_.copy(up_shard.at[:, unit_columns(x, number)], up_all.at[z, y, x, :, window]))
+    later.append(locals_.copy(down_shard.at[pl.ds(pl.multiple_of(rep * unit, 16), unit)], down_all.at[z, y]))
     grad_load = locals_.copy(grad_out, grad_in)
-    half = down_all.shape[-2]
-    staged.append(locals_.copy(down_shard.at[pl.ds(pl.multiple_of(rep * half, 16), half)], down_all.at[z, y, x]))
-    for block in range(up_all.shape[-1] // half):
-        begin = pl.multiple_of((2 * block + rep) * half, half)
-        staged.append(locals_.copy(
-            up_shard.at[:, pl.ds(begin, half)], up_all.at[z, y, x, :, pl.ds(block * half, half)]))
     latents_load = locals_.copy(latents, latents_in)
     media_load = locals_.copy(media, media_in)
     links.greet()
-    for copy in staged:
-        copy.wait()
 
     def halves(whole, begin, size, order):
         def view(zi, yi, xi, half=rep):
@@ -318,24 +362,30 @@
 
         return Gather(links, slots, view, order, True)
 
-    def columns(whole, begin, size, order):
-        return Gather(links, slots, lambda zi, yi, xi: whole.at[zi, yi, xi, :, pl.ds(begin, size)], order, False)
-
     gathers = [
-        [Gather(links, slots, lambda zi, yi, xi: packed_all.at[zi, yi, xi], xy, False),
-         halves(context_all, 0, width // 2, xy), halves(context_all, width // 2, width // 2, yx)],
-        [halves(query_all, 0, inner, xy), halves(output_all, 0, width, yx)],
+        (Gather(links, slots, lambda zi, yi, xi: packed_all.at[zi, yi, xi], xy, False), 0, 1),
+        (halves(context_all, 0, width // 2, xy), 0, 1), (halves(context_all, width // 2, width // 2, yx), 0, 1),
+        (halves(query_all, 0, inner, xy), 1, 1), (halves(output_all, 0, width, yx), 1, 1),
     ]
-    for whole in (down_all, up_all):
-        part = whole.shape[-1] // (2 * chunks)
-        for number in range(chunks):
-            gathers.append(
-                [columns(whole, 2 * number * part, part, xy), columns(whole, (2 * number + 1) * part, part, yx)])
+    for number in range(chunks):
+        window = pl.ds(number * (width // chunks), width // chunks)
+        gathers.append((Gather(links, slots, lambda zi, yi, xi, window=window: down_all.at[zi, yi, :, window],
+                               ("z", "y"), False), 2 + number, 2))
+    for number in range(chunks):
+        window = pl.ds(number * chunk, chunk)
+        gathers.append((Gather(links, slots, lambda zi, yi, xi, window=window: up_all.at[zi, yi, ALL, :, window],
+                               ("z", "y"), False), 2 + chunks + number, 2))
+    up_across = slots.move(links.device("x"), up_stage, up_all.at[z, y, x], up_all.at[z, y, 1 - x])
     gathered = len(slots.made)
+    parts = [(0, 2 * latent_count), (2 * latent_count, rows - 2 * latent_count)]
+    branch_rows = Rows(links, slots, branch, rows, [(0, rows)])
+    feed_rows = Rows(links, slots, feed, rows, parts)
 
     def pump(tick):
-        run(gathers, 5, tick)
-
+        run(gathers, tick)
+
+    for copy in staged:
+        copy.wait()
     pump(0)
     grad_load.wait()
     count = counts[0]
@@ -345,15 +395,15 @@
 
     for j in range(slot_count):
         branch[pl.ds(j * latent_count, latent_count)] = (grad_in[j].astype(F32) * keep(j)).astype(BF16)
-    branch_move = slots.move(links.device("core"), branch.at[pl.ds(0, rows)], branch.at[pl.ds(rows, rows)],
-                             branch.at[pl.ds(rows, rows)])
-    branch_move.start()
     mask[...] = head_mask(latent_count, GROUP)
     sums[...] = jnp.zeros_like(sums)
+    for copy in later:
+        copy.wait()
     pump(1)
+    up_across.start()
+    pump(2)
     latents_load.wait()
     media_load.wait()
-    pump(2)
     pump(3)
     lane = packed_all.shape[-1]
     for zi in range(length):
@@ -377,22 +427,19 @@
 
     pl.loop(0, slot_count)(normalise_slot)
     pump(4)
-
-    weight_step = 256
+    branch_rows.send(0)
 
     def key_value_slot(j):
-        def body(at):
-            weight = context_all[:, :, :, :, :, pl.ds(at, weight_step)].reshape(width, weight_step)
-            key_value[j, :, pl.ds(at, weight_step)] = matmul(context[j], weight).astype(BF16)
-
-        tiles(width // weight_step, weight_step, body)
-
-    pl.loop(0, slot_count)(key_value_slot)
+        key_value[j] = matmul(context[j], context_all[...].reshape(width, 2 * inner)).astype(BF16)
+
+    pl.loop(0, 3)(key_value_slot)
     pump(5)
-
+    pl.loop(3, slot_count)(key_value_slot)
     latent_normed = context[:, patches:, :].reshape(rows, width)
     query[...] = (matmul(latent_normed, query_all[...].reshape(width, inner)) * scaling).astype(BF16).reshape(
         slot_count, latent_count, inner)
+    up_across.wait()
+    pump(6)
 
     def attention_slot(j):
         for begin in range(0, inner, GROUP):
@@ -401,131 +448,161 @@
             value = matmul(probs, key_value[j, :, inner + begin:inner + begin + GROUP])
             attended[j, :, begin:begin + GROUP] = pick_heads(value, mask[...], latent_count).astype(BF16)
 
-    pl.loop(0, slot_count)(attention_slot)
-    pump(6)
-
-    def output_tile(at):
-        weight = output_all[:, :, :, :, :, pl.ds(at, weight_step)].reshape(inner, weight_step)
-        after[:, pl.ds(at, weight_step)] = latents_in[:, :, pl.ds(at, weight_step)].reshape(
-            rows, weight_step).astype(F32) + matmul(attended[...].reshape(rows, inner), weight)
-
-    tiles(width // weight_step, weight_step, output_tile)
-
     def feed_tile(at):
         feed[pl.ds(at, step)] = layer_norm(after[pl.ds(at, step)], vectors[4:5], vectors[5:6]).astype(BF16)
 
-    tiles(rows // step, step, feed_tile)
-    feed_move = slots.move(links.device("core"), feed.at[pl.ds(0, rows)], feed.at[pl.ds(rows, rows)],
-                           feed.at[pl.ds(rows, rows)])
-    feed_move.start()
-    pump(7)
-    branch_move.wait()
-
-    def turn(source, target):
+    for part, (begin, size) in enumerate(parts):
+        first, last = begin // latent_count, (begin + size) // latent_count
+        pl.loop(first, last)(attention_slot)
+        after[begin:begin + size] = latents_in[first:last].reshape(size, width).astype(F32) + matmul(
+            attended[first:last].reshape(size, inner), output_all[...].reshape(inner, width))
+        pl.loop(begin // step, (begin + size) // step)(lambda n: feed_tile(pl.multiple_of(n * step, step)))
+        feed_rows.send(part)
+        pump(7 + part)
+    branch_rows.near(0)
+    branch_rows.forward(0)
+    pump(9)
+    branch_rows.far(0)
+
+    def turn(source, target, owner):
         def body(at):
-            target[pl.ds(at, weight_step)] = source[:, pl.ds(at, weight_step)].T
-
-        tiles(width // weight_step, weight_step, body)
-
-    turn(branch, branch_t)
-    feed_move.wait()
-    turn(feed, feed_t)
-    pump(8)
+            target[pl.ds(at, 256), pl.ds(owner * rows, 2 * rows)] = source[
+                pl.ds(owner * rows, 2 * rows), pl.ds(at, 256)].T
+
+        tiles(width // 256, 256, body)
+
     tall = rows
-    short = 128
-
-    def reduction(own, lands, windows, order, keep_total):
-        return Reduce(links, slots, own, order, lands[0].at[(ALL, ALL) + windows], lands[1].at[(ALL,) + windows],
-                      lands[2].at[(ALL,) + windows], keep_total)
-
-    def halved_reduction(own, lands, target, height, begin, size, along_rows):
-        made = []
-        for which, order in enumerate((yx, xy)):
-            window = pl.ds(begin + which * size, size)
-            windows = (window, pl.ds(0, target.shape[1])) if along_rows else (pl.ds(0, height), window)
-
-            def finish(value, windows=windows):
-                target[windows] = value
-
-            made.append(reduction(lambda zi, yi, xi, windows=windows: own(zi, yi, xi, *windows), lands, windows, order, finish))
-        return made
-
-    up_lands, down_lands, query_lands, context_lands, output_lands = zip(lands_b, lands_a, lands_z)
+    d_active, active, d_hidden = [pool.at[pl.ds(n * 4 * rows, 4 * rows)] for n in range(3)]
+
+    def d_active_tile(at):
+        d_active[pl.ds(at, tall)] = matmul_right(
+            branch[pl.ds(at, tall)], down_all[...].reshape(hidden, width)).astype(BF16)
+
+    tiles(4, tall, d_active_tile)
+    turn(branch, branch_t, 0)
+    turn(branch, branch_t, 2)
+    pump(10)
+    feed_rows.forward(0)
+    feed_rows.near(0)
+    feed_rows.near(1)
+
+    def hidden_tile(at, begin):
+        window = pl.ds(begin, chunk)
+        weight = up_all[:, :, :, :, window].reshape(width, chunk)
+        value, slope = gelu_parts(matmul(feed[pl.ds(at, tall)], weight))
+        active[pl.ds(at, tall), window] = value.astype(BF16)
+        d_hidden[pl.ds(at, tall), window] = (d_active[pl.ds(at, tall), window].astype(F32) * slope).astype(BF16)
+
+    for c in range(chunks):
+        tiles(2, tall, lambda at, c=c: hidden_tile(at, c * chunk))
+        if c == 0:
+            feed_rows.forward(1)
+            turn(feed, feed_t, 0)
+        pump(11 + c)
+    feed_rows.far(0)
+    feed_rows.far(1)
+    for move in slots.made[:gathered]:
+        move.drain()
+    feed_rows.drain()
+    branch_rows.drain()
+    d_feed_back = Partials(links, slots, feed, d_feed_lands, rows)
+    after_back = Partials(links, slots, branch, after_lands, rows)
+    turn(feed, feed_t, 2)
+
+    def far_tile(at):
+        pl.loop(0, chunks)(lambda c: hidden_tile(pl.multiple_of(2 * rows + at, tall), pl.multiple_of(c * chunk, chunk)))
+
+    tiles(2, tall, far_tile)
+
+    def d_feed_of(owner):
+        return matmul_right(d_hidden[pl.ds(owner * rows, rows)], up_all[...].reshape(width, hidden))
+
+    def after_feed_of(owner):
+        return matmul(active[pl.ds(owner * rows, rows)], down_all[...].reshape(hidden, width))
+
+    def rounded(buffer, owner, value):
+        buffer[pl.ds(owner * rows, rows)] = value.astype(BF16)
+
+    rounded(feed, 3, d_feed_of(3))
+    d_feed_back.far.start()
+    totals[1] = d_feed_of(2)
+    d_feed_back.far.wait()
+
+    def across_tile(back, buffer):
+        def body(at):
+            here = pl.ds(at, step)
+            buffer[pl.ds(2 * rows + at, step)] = (totals[1, here] + back.lands[0, here].astype(F32)).astype(BF16)
+
+        tiles(rows // step, step, body)
+
+    across_tile(d_feed_back, feed)
+    d_feed_back.across.start()
+    rounded(feed, 1, d_feed_of(1))
+    d_feed_back.near.start()
+    totals[0] = d_feed_of(0)
+
     up_result, down_result, query_result, context_result, output_result = result
     reductions = []
 
     def send_off(tick):
-        run(reductions, 4, tick)
+        run(reductions, tick)
+
+    def plane_reduction(own, lands_y, lands, finish):
+        return Reduce(links, slots, own, ("y",), [lands_y], lands, finish)
+
+    def keep_up(value, window):
+        up_result[0, :, window] = jnp.where(x == 0, value[0], value[1])
+        own_rows_send[:, window] = jnp.where(x == 0, value[1], value[0]).astype(BF16)
 
     for c in range(chunks):
-        def d_active_tile(at, c=c):
-            weight = down_all[c].reshape(chunk, width)
-            pool[pl.ds(c * both + at, tall)] = matmul_right(branch[pl.ds(at, tall)], weight).astype(BF16)
-
-        tiles(both // tall, tall, d_active_tile)
-    d_hidden = pool.at[pl.ds(chunks * both, both)]
-    for c in range(chunks):
-        pump(9 + c)
         begin = c * chunk
-
-        def hidden_tile(at, c=c, begin=begin):
-            weight = up_all[:, :, :, :, begin:begin + chunk].reshape(width, chunk)
-            value, slope = gelu_parts(matmul(feed[pl.ds(at, short)], weight))
-            active[pl.ds(at, short)] = value.astype(BF16)
-            d_hidden[pl.ds(at, short)] = (pool[pl.ds(c * both + at, short)].astype(F32) * slope).astype(BF16)
-
-        tiles(both // short, short, hidden_tile)
-
-        def forward_tile(at, c=c):
-            value = matmul(active[pl.ds(at, tall)], down_all[c].reshape(chunk, width))
-            after_feed[pl.ds(at, tall)] = value if c == 0 else after_feed[pl.ds(at, tall)] + value
-
-        def back_tile(at, c=c, begin=begin):
-            weight = up_all[:, :, :, :, begin:begin + chunk].reshape(width, chunk)
-            value = matmul_right(d_hidden[pl.ds(at, tall)], weight)
-            d_feed[pl.ds(at, tall)] = value if c == 0 else d_feed[pl.ds(at, tall)] + value
-
-        tiles(both // tall, tall, forward_tile)
-        tiles(both // tall, tall, back_tile)
-        if c == chunks - 1:
-            for move in slots.made[:gathered]:
-                move.drain()
-            d_feed_move = slots.move(links.device("core"), d_feed.at[pl.ds(rows, rows)], d_feed_lands, d_feed_lands)
-            after_move = slots.move(links.device("core"), after_feed.at[pl.ds(rows, rows)], after_lands, after_lands)
-            d_feed_move.start()
-            after_move.start()
-
-        def grad_tile(zi, begin=begin, c=c):
-            place = pl.multiple_of(zi * (width // length), width // length)
-            up = matmul(feed_t[pl.ds(place, width // length)], d_hidden[...]).astype(BF16)
-            grad_up[zi, :, :, :, begin:begin + chunk] = up.reshape(2, 2, width // (4 * length), chunk)
-            down = matmul(branch_t[pl.ds(place, width // length)], active[...]).astype(BF16)
-            block = chunk // 4
-            for number in range(4):
-                grad_down[c, number // 2, number % 2, pl.ds(place, width // length)] = down[
-                    :, number * block:(number + 1) * block]
-
-        pl.loop(0, length)(grad_tile)
-        reductions.append(halved_reduction(
-            lambda zi, yi, xi, *w: grad_up.at[(zi, yi, xi) + w], up_lands, up_result, up_result.shape[0],
-            begin, chunk // 2, False))
+        window = pl.ds(begin, chunk)
+
+        def grad_tile(number, window=window, c=c):
+            size = width // 2
+            place = pl.multiple_of(number * size, size)
+            up = matmul(feed_t[pl.ds(place, size)], d_hidden[:, window]).astype(BF16)
+            grad_up[pl.ds(number * (length // 2), length // 2), :, :, :, window] = up.reshape(
+                length // 2, 2, 2, size // (2 * length), chunk)
+            down = matmul(branch_t[pl.ds(place, size)], active[:, window]).astype(BF16)
+            for owner in range(2):
+                grad_down[c, owner, pl.ds(place, size)] = down[:, owner * unit:(owner + 1) * unit]
+
+        pl.loop(0, 2)(grad_tile)
+        reductions.append((plane_reduction(
+            lambda zi, yi, xi, window=window: grad_up.at[zi, yi, ALL, :, window],
+            lands_b[0].at[:, :, :, window], lands_z[0].at[:, :, :, window],
+            functools.partial(keep_up, window=window)), c, 2))
         send_off(c)
-    part = width // chunks
+    part_size = width // chunks
     for number in range(chunks):
-        reductions.append(halved_reduction(
-            lambda zi, yi, xi, *w: grad_down.at[(zi, yi, xi) + w], down_lands, down_result, width,
-            number * part, part // 2, True))
-
-    d_feed_move.wait()
-    feed_move.drain()
+        window = pl.ds(number * part_size, part_size)
+
+        def keep_down(value, window=window):
+            down_result[window] = value
+
+        reductions.append((plane_reduction(
+            lambda zi, yi, xi, window=window: grad_down.at[zi, yi, window],
+            lands_b[1].at[:, window], lands_z[1].at[:, window], keep_down), chunks + number, 2))
+
+    rounded(branch, 3, after_feed_of(3))
+    after_back.far.start()
+    d_feed_back.near.wait()
+    d_feed_back.across.wait()
+    send_off(4)
 
     def fold(terms):
         return jnp.sum(terms.reshape(-1, 8, width), axis=0)
+
+    d_feed = totals.at[0]
+    d_feed_back.far.drain()
+    d_feed_back.near.drain()
+    d_feed_back.across.drain()
 
     def middle_slot(j):
         def body(at):
             own = pl.ds(pl.multiple_of(j * latent_count + at, step), step)
-            upstream = d_feed[own] + d_feed_lands[own]
+            upstream = d_feed[own] + d_feed_lands[1, own].astype(F32) + d_feed_lands[2, own].astype(F32)
             d_norm, gain_terms = layer_norm_back(after[own], vectors[4:5], upstream)
             sums[4] = sums[4] + fold(gain_terms)
             sums[5] = sums[5] + fold(upstream)
@@ -536,58 +613,66 @@
         tiles(latent_count // step, step, body)
 
     pl.loop(0, slot_count)(middle_slot)
-    send_off(4)
-    after_move.wait()
-    for j in range(slot_count):
-        own = pl.ds(j * latent_count, latent_count)
-        out_stage[j] = ((after[own] + after_feed[own] + after_lands[own]) * keep(j)).astype(BF16)
-    written = [locals_.copy(out_stage, latents_out)]
-
-    output_rows, context_rows = output_all.shape[-2], context_all.shape[-2]
-    output_at = 3 * down_all.shape[-2] // 4
-
-    def output_own(zi, yi, xi, half, *w):
-        return down_all.at[zi, yi, xi, pl.ds(pl.multiple_of(output_at + half * output_rows, 16), output_rows), w[1]]
-
-    def context_own(zi, yi, xi, half, *w):
-        return up_all.at[zi, yi, xi, pl.ds(pl.multiple_of(half * context_rows, 16), context_rows), w[1]]
-
-    def query_own(zi, yi, xi, half, *w):
-        moved = pl.ds(2 * inner + w[1].start, w[1].size)
-        return up_all.at[zi, yi, xi, pl.ds(pl.multiple_of(half * context_rows, 16), context_rows), moved]
-
-    sibling_lands = {
-        "context": down_all.at[:, :, :, pl.ds(0, context_rows)],
-        "query": down_all.at[:, :, :, pl.ds(context_rows, context_rows), pl.ds(0, inner)],
-        "output": down_all.at[:, :, :, pl.ds(2 * context_rows, output_rows)],
-    }
-
-    def to_sibling(own, name, size):
-        whole = (None, pl.ds(0, size))
-        move = slots.move(links.device("core"), own(ALL, ALL, ALL, 1 - rep, *whole), sibling_lands[name],
-                          sibling_lands[name])
+    totals[1] = after_feed_of(2)
+    after_back.far.wait()
+    across_tile(after_back, branch)
+    after_back.across.start()
+    rounded(branch, 1, after_feed_of(1))
+    after_back.near.start()
+    after[...] = after[...] + after_feed_of(0)
+    send_off(5)
+
+    context_rows, output_rows = context_all.shape[-2], output_all.shape[-2]
+
+    def context_own(zi, yi, xi, half):
+        return up_all.at[zi, yi, xi, pl.ds(pl.multiple_of(half * context_rows, 16), context_rows)]
+
+    def query_own(zi, yi, xi, half):
+        return grad_query.at[zi, yi, xi, half]
+
+    def output_own(zi, yi, xi, half):
+        return grad_output.at[zi, yi, xi, half]
+
+    def to_sibling(own, land):
+        move = slots.move(links.device("core"), own(ALL, ALL, ALL, 1 - rep), land, land)
         move.start()
 
         def settle():
             move.wait()
-            add_into(own(ALL, ALL, ALL, rep, *whole), sibling_lands[name])
+            add_into(own(ALL, ALL, ALL, rep), land)
 
         return settle
 
+    def halved_reduction(own, number, target, first):
+        made = []
+        size = target.shape[-1] // 2
+        for which, order in enumerate((("y", "x"), ("x", "y"))):
+            window = pl.ds(which * size, size)
+
+            def finish(value, window=window):
+                target[:, window] = value
+
+            made.append((Reduce(
+                links, slots, lambda zi, yi, xi, window=window: own(zi, yi, xi, rep).at[..., window], order,
+                [lands_b[number].at[:, :, :, window], lands_a[number].at[:, :, window]],
+                lands_z[number].at[:, :, window], finish), first, 1))
+        return made
+
     d_branch = feed.at[pl.ds(0, rows)]
-    output_block = inner // length
-
-    def output_grad_tile(zi):
-        place = pl.multiple_of(zi * output_block, output_block)
+    output_block = inner // 2
+
+    def output_grad_tile(number):
+        place = pl.multiple_of(number * output_block, output_block)
         turned = attended[:, :, pl.ds(place, output_block)].reshape(rows, output_block).T
         value = matmul(turned, d_branch[...]).astype(BF16)
-        down_all[zi, :, :, output_at:] = value.reshape(2, 2, output_block // 4, width)
-
-    pl.loop(0, length)(output_grad_tile)
-    settle_output = to_sibling(output_own, "output", width)
-    d_attended, d_query = active.at[pl.ds(0, rows)], active.at[pl.ds(rows, rows)]
+        grad_output[pl.ds(number * (length // 2), length // 2)] = value.reshape(
+            length // 2, 2, 2, 2, output_rows, width)
+
+    pl.loop(0, 2)(output_grad_tile)
+    settle_output = to_sibling(output_own, lands_c[2])
+    d_attended, d_query = upstream_rows[0], upstream_rows[1]
     d_attended[...] = matmul_right(d_branch[...], output_all[...].reshape(inner, width)).astype(BF16)
-    send_off(5)
+    send_off(6)
 
     def attention_back_slot(j):
         own = pl.ds(pl.multiple_of(j * latent_count, latent_count), latent_count)
@@ -603,74 +688,71 @@
             d_query[own, begin:begin + GROUP] = (
                 pick_heads(matmul(d_scores, keys), mask[...], latent_count).astype(BF16).astype(F32) * scaling
             ).astype(BF16)
-            at = pl.multiple_of(j * 2 * key_count, 16)
-            pool[pl.ds(at, key_count), begin:begin + GROUP] = matmul_left(d_scores, stacked).astype(BF16)
-            pool[pl.ds(at + key_count, key_count), begin:begin + GROUP] = matmul_left(
-                probs.astype(BF16), upstream).astype(BF16)
+            at = pl.ds(pl.multiple_of(j * key_count, 16), key_count)
+            pool[at, begin:begin + GROUP] = matmul_left(d_scores, stacked).astype(BF16)
+            pool[at, inner + begin:inner + begin + GROUP] = matmul_left(probs.astype(BF16), upstream).astype(BF16)
 
     pl.loop(0, 2)(attention_back_slot)
-    send_off(6)
+    send_off(7)
     pl.loop(2, slot_count)(attention_back_slot)
-    send_off(7)
-
+    send_off(8)
     block = width // length
 
     def query_grad_tile(zi):
         place = pl.multiple_of(zi * block, block)
         turned = context[:, patches:, pl.ds(place, block)].reshape(rows, block).T
         value = matmul(turned, d_query[...]).astype(BF16)
-        up_all[zi, :, :, :, 2 * inner:3 * inner] = value.reshape(2, 2, block // 4, inner)
+        grad_query[zi] = value.reshape(2, 2, 2, context_rows, inner)
 
     pl.loop(0, length)(query_grad_tile)
-    settle_query = to_sibling(query_own, "query", inner)
+    settle_query = to_sibling(query_own, lands_c[0])
 
     def context_grad_tile(zi):
         place = pl.multiple_of(zi * block, block)
-        for which in range(2):
-            value = None
-            for j in range(slot_count):
-                turned = context[j, :, pl.ds(place, block)].T
-                at = (2 * j + which) * key_count
-                term = matmul(turned, pool[at:at + key_count])
-                value = term if value is None else value + term
-            up_all[zi, :, :, :, which * inner:(which + 1) * inner] = value.astype(BF16).reshape(
-                2, 2, block // 4, inner)
-
-    pl.loop(0, length)(context_grad_tile)
-    settle_context = to_sibling(context_own, "context", width)
+        value = None
+        for j in range(slot_count):
+            turned = context[j, :, pl.ds(place, block)].T
+            term = matmul(turned, pool[j * key_count:(j + 1) * key_count])
+            value = term if value is None else value + term
+        up_all[zi] = value.astype(BF16).reshape(2, 2, block // 4, 2 * inner)
+
+    pl.loop(0, 2)(context_grad_tile)
+    send_off(9)
+    pl.loop(2, length)(context_grad_tile)
+    settle_context = to_sibling(context_own, lands_c[1])
     settle_output()
     settle_query()
-    reductions.append(
-        halved_reduction(lambda zi, yi, xi, *w: output_own(zi, yi, xi, rep, *w), output_lands, output_result,
-                         output_rows, 0, width // 2, False)
-        + halved_reduction(lambda zi, yi, xi, *w: query_own(zi, yi, xi, rep, *w), query_lands, query_result,
-                           context_rows, 0, inner // 2, False))
-    send_off(8)
+    first = 2 * chunks + 2
+    reductions.extend(halved_reduction(output_own, 4, output_result, first))
+    reductions.extend(halved_reduction(query_own, 2, query_result, first))
+    send_off(10)
     settle_context()
-    reductions.append(halved_reduction(
-        lambda zi, yi, xi, *w: context_own(zi, yi, xi, rep, *w), context_lands, context_result, context_rows,
-        0, width // 2, False))
-    send_off(9)
-
-    upstream_rows = d_feed_lands
+    reductions.extend(halved_reduction(context_own, 3, context_result, first + 1))
+    send_off(11)
+    own_rows_move = slots.move(links.device("x"), own_rows_send, own_rows_land, own_rows_land)
+    own_rows_move.start()
+    after_back.near.wait()
+    after_back.across.wait()
+    for move in (after_back.far, after_back.near, after_back.across):
+        move.drain()
+    for j in range(slot_count):
+        own = pl.ds(j * latent_count, latent_count)
+        branch[own] = ((after[own] + after_lands[1, own].astype(F32) + after_lands[2, own].astype(F32))
+                       * keep(j)).astype(BF16)
+    written = [locals_.copy(branch.at[pl.ds(j * latent_count, latent_count)], latents_out.at[j])
+               for j in range(slot_count)]
+
+    context_up = totals.at[1]
 
     def input_slot(j):
-        at = pl.multiple_of(j * 2 * key_count, 16)
-
-        def upstream_tile(number):
-            weight = context_all[number].reshape(block, 2 * inner)
-            place = pl.ds(pl.multiple_of(number * block, block), block)
-            upstream_rows[:, place] = (matmul_right(pool[pl.ds(at, key_count)], weight[:, :inner])
-                                       + matmul_right(pool[pl.ds(at + key_count, key_count)], weight[:, inner:]))
-            own = pl.ds(pl.multiple_of(j * latent_count, latent_count), latent_count)
-            upstream_rows[patches:, place] = upstream_rows[patches:, place] + matmul_right(
-                d_query[own], query_all[number].reshape(block, inner))
-
-        pl.loop(0, length)(upstream_tile)
+        at = pl.ds(pl.multiple_of(j * key_count, 16), key_count)
+        own = pl.ds(pl.multiple_of(j * latent_count, latent_count), latent_count)
+        context_up[...] = matmul_right(pool[at], context_all[...].reshape(width, 2 * inner))
+        context_up[patches:] = context_up[patches:] + matmul_right(d_query[own], query_all[...].reshape(width, inner))
 
         def media_tile(at):
             own = pl.ds(at, step)
-            upstream = upstream_rows[own]
+            upstream = context_up[own]
             value, gain_terms = layer_norm_back(media_in[j, own].astype(F32), vectors[0:1], upstream)
             sums[0] = sums[0] + fold(gain_terms)
             sums[1] = sums[1] + fold(upstream)
@@ -678,7 +760,7 @@
 
         def latent_tile(at):
             own = pl.ds(at, step)
-            upstream = upstream_rows[pl.ds(patches + at, step)]
+            upstream = context_up[pl.ds(patches + at, step)]
             value, gain_terms = layer_norm_back(latents_in[j, own].astype(F32), vectors[2:3], upstream)
             sums[2] = sums[2] + fold(gain_terms)
             sums[3] = sums[3] + fold(upstream)
@@ -689,8 +771,13 @@
         tiles(latent_count // step, step, latent_tile)
 
     pl.loop(0, 2)(input_slot)
-    send_off(10)
-    pl.loop(2, slot_count)(input_slot)
+    send_off(12)
+    own_rows_move.wait()
+    up_result[1] = own_rows_land[...].astype(F32)
+    pl.loop(2, 3)(input_slot)
+    send_off(13)
+    pl.loop(3, slot_count)(input_slot)
+    send_off(14)
     written.append(locals_.copy(media_in, media_grad_out))
     written.append(locals_.copy(latents_in, latents_grad_out))
     total[...] = jnp.zeros_like(total)
@@ -698,22 +785,19 @@
         total[number:number + 1] = jnp.sum(sums[number], axis=0, keepdims=True)
     vector_sum = VectorSum(links, slots, total, total_stage, total_lands)
     vector_sum.step(0)
-    send_off(11)
-    vector_sum.step(1)
-    send_off(12)
-    for number in range(2, 5):
-        vector_sum.step(number)
-    sums_out[...] = total[...]
+    send_off(15)
     for value, out in zip(result, grads_out):
         written.append(locals_.copy(value, out.at[rep]))
         move = slots.move(links.device("core"), value, out.at[rep], out.at[1 - rep])
         move.start()
         written.append(move)
+    for number in range(1, 5):
+        vector_sum.step(number)
+    sums_out[...] = total[...]
     for copy in written:
         copy.wait()
-    drained = slots.made[gathered:]
-    for move in drained:
-        if move is not feed_move:
+    for move in slots.made:
+        if not move.drained:
             move.drain()
 
 
@@ -724,16 +808,17 @@
     key_count = patches + latent_count
     rows = slot_count * latent_count
     inner = query_shard.shape[1]
-    hidden = up_shard.shape[1] // 2
-    chunk = hidden // length
+    unit = down_shard.shape[0] // 2
+    hidden = up_shard.shape[1] // 4
     blocks = (length, 2, 2)
 
     def halved(shard):
         return blocks + (2, shard.shape[0] // 2, shard.shape[1])
 
-    grad_up_shape = blocks + (up_shard.shape[0], hidden)
-    grad_down_shape = blocks + (width, down_shard.shape[0] // 2)
-    results = [grad_up_shape[3:], grad_down_shape[3:]] + [halved(s)[4:] for s in shards[:3]]
+    up_shape = blocks + (up_shard.shape[0], hidden)
+    down_shape = (length, 2, unit, width)
+    halves = [halved(s)[4:] for s in shards[:3]]
+    results = [(2,) + up_shape[3:], (width, unit)] + halves
     anywhere = pl.BlockSpec(memory_space=pl.ANY)
     vmem = pl.BlockSpec(memory_space=pltpu.VMEM)
     sums_shape = (8, width)
@@ -741,8 +826,9 @@
         pltpu.VMEM(halved(query_shard), BF16),
         pltpu.VMEM(halved(context_shard), BF16),
         pltpu.VMEM(halved(output_shard), BF16),
-        pltpu.VMEM(grad_up_shape, BF16),
-        pltpu.VMEM(blocks + (down_shard.shape[0] // 2, width), BF16),
+        pltpu.VMEM(up_shape, BF16),
+        pltpu.VMEM(up_shape[3:], BF16),
+        pltpu.VMEM(down_shape, BF16),
         pltpu.VMEM(blocks + packed.shape, BF16),
         pltpu.VMEM((8, width), F32),
         pltpu.VMEM(media.shape, BF16),
@@ -753,30 +839,35 @@
         pltpu.VMEM((slot_count, latent_count, inner), BF16),
         pltpu.VMEM((slot_count, latent_count, inner), BF16),
         pltpu.VMEM((rows, width), F32),
-        pltpu.VMEM((2 * rows, width), BF16),
-        pltpu.VMEM((width, 2 * rows), BF16),
-        pltpu.VMEM((2 * rows, width), BF16),
-        pltpu.VMEM((width, 2 * rows), BF16),
-        pltpu.VMEM((max((length + 1) * 2 * rows, 2 * slot_count * key_count), chunk), BF16),
-        pltpu.VMEM((2 * rows, chunk), BF16),
-        pltpu.VMEM((2 * rows, width), F32),
-        pltpu.VMEM((2 * rows, width), F32),
-        pltpu.VMEM((rows, width), F32),
-        pltpu.VMEM((rows, width), F32),
-        pltpu.VMEM(latents.shape, BF16),
-        pltpu.VMEM(grad_up_shape, BF16),
-        pltpu.VMEM(grad_down_shape, BF16),
+        pltpu.VMEM((4 * rows, width), BF16),
+        pltpu.VMEM((width, 4 * rows), BF16),
+        pltpu.VMEM((4 * rows, width), BF16),
+        pltpu.VMEM((width, 4 * rows), BF16),
+        pltpu.VMEM((max(12 * rows, slot_count * key_count), hidden), BF16),
+        pltpu.VMEM((2, rows, width), F32),
+        pltpu.VMEM((3, rows, width), BF16),
+        pltpu.VMEM((3, rows, width), BF16),
+        [pltpu.VMEM((rows, inner), BF16)] * 2,
+        pltpu.VMEM(up_shape, BF16),
+        pltpu.VMEM((length, 2, width, unit), BF16),
+        pltpu.VMEM(halved(query_shard), BF16),
+        pltpu.VMEM(halved(output_shard), BF16),
         pltpu.VMEM((latent_count * (GROUP // HEAD_DIM), GROUP), F32),
         pltpu.VMEM((6, 8, width), F32),
         pltpu.VMEM(sums_shape, F32),
         pltpu.VMEM((4,) + sums_shape, F32),
         pltpu.VMEM((2 + length,) + sums_shape, F32),
-        [pltpu.VMEM((length, 2) + r, BF16) for r in results],
-        [pltpu.VMEM((length,) + r, BF16) for r in results],
-        [pltpu.VMEM((length - 1,) + r, BF16) for r in results],
+        pltpu.VMEM(up_shape[3:], BF16),
+        pltpu.VMEM(up_shape[3:], BF16),
+        [pltpu.VMEM(blocks + h, BF16) for h in halves],
+        [pltpu.VMEM((length, 2) + up_shape[3:], BF16), pltpu.VMEM((length, width, unit), BF16)]
+        + [pltpu.VMEM((length, 2) + h, BF16) for h in halves],
+        [None, None] + [pltpu.VMEM((length,) + h, BF16) for h in halves],
+        [pltpu.VMEM((length - 1, 2) + up_shape[3:], BF16), pltpu.VMEM((length - 1, width, unit), BF16)]
+        + [pltpu.VMEM((length - 1,) + h, BF16) for h in halves],
         [pltpu.VMEM(r, F32) for r in results],
-        pltpu.SemaphoreType.DMA((240,)),
-        pltpu.SemaphoreType.DMA((240,)),
+        pltpu.SemaphoreType.DMA((200,)),
+        pltpu.SemaphoreType.DMA((200,)),
         pltpu.SemaphoreType.DMA((64,)),
     ]
     out_shape = (
@@ -977,10 +1068,11 @@
     latents_out, grad_media, grad_latents, vector_sums, summed = layer(
         chips // 4, image_counts, media[0], latents[0], grad_out[0], packed, weight_shards)
     sums = [s.reshape(-1, s.shape[-1]) for s in summed[2:]]
-    rows, hidden = summed[0].shape[1:]
-    half = summed[1].shape[-1]
-    sums.append(summed[0].reshape(2, rows, hidden // half, half).transpose(1, 2, 0, 3).reshape(rows, 2 * hidden))
-    sums.append(summed[1].transpose(0, 2, 1).reshape(2 * half, -1))
+    rows, hidden = summed[0].shape[2:]
+    unit = summed[1].shape[-1]
+    planes = jnp.where(lax.rem(lax.axis_index("dp"), 2) == 0, summed[0], summed[0][:, ::-1])
+    sums.append(planes.reshape(2, 2, rows, hidden // unit, unit).transpose(2, 3, 1, 0, 4).reshape(rows, 4 * hidden))
+    sums.append(summed[1].transpose(0, 2, 1).reshape(2 * unit, -1))
     width = parameters[0].shape[0]
     mine = lax.dynamic_slice(vector_sums, (0, lax.axis_index("dp") * width), (6, width))
     return (latents_out[None], grad_media[None], grad_latents[None]) + tuple(mine) + tuple(sums)

time: 251 us -> 211 us (0.84)
  Pallas kernels: 235 us -> 194 us
    pallas_call x1, Pallas kernels: 235 us -> 194 us  [layer(): pl.pallas_call(functools.partial(layer_kernel, length, HEAD_DIM ** (-0.5)...]
where the time goes in v1:
time: 211 us
  Pallas kernels  194 us (92%)
  local copies, waits for them, and re-layouts  12.7 us (6%)
  other arithmetic  2.4 us (1%)
    pallas_call x1, Pallas kernels, layer(): pl.pallas_call(functools.partial(layer_kernel, length, HEAD_DIM ** (-0.5)...  194 us
    unnamed x19, local copies, waits for them, and re-layouts  5.4 us

profile of v1, /device:TPU:0, one launch (start us, length us, event | category | flops | bytes accessed | tf_op | source)
XLA Modules:
  0.0 210.8 jit_solution(18017177082666046390)
XLA Ops:
  0.7 0.8 stack.27
  1.4 0.7 fusion.2.packed
  2.7 194.3 %resampler_layer.1 = (bf16[5,64,1024]{2,1,0:T(8,128)(2,1)}, bf16[5,256,1024]{2,1,0:T(8,128)(2,1)}, bf16[5,64,1024]{2,1,0:T(8,128)(2,1)}, f32[8,1024]{1,0:T(8,128...) custom-call(s32[1]{0:T(128)S(6)} %copy.39.counts, ...), custom_call_target="tpu_custom_call" | custom-call | tf_op jit(solution)/shard_map/resampler_layer/pallas_call | solution.py:877
  197.0 1.7 reverse_select_fusion
  198.8 0.2 copy.32
  199.0 0.8 copy.30
  199.8 0.0 copy-start.2
  199.8 1.8 reshape.50
  201.6 0.0 copy-start
  201.6 0.9 constant_dynamic-slice_fusion
  202.5 0.5 slice_bitcast_fusion
  203.0 2.5 %copy.31 = f32[2,128,1024]{2,1,0:T(8,128)} copy(f32[2,128,1024]{1,2,0:T(8,128)} %bitcast.40) | data formatting | bytes 2097152 | tf_op jit(solution)/shard_map/transpose | solution.py:1075
  205.6 0.0 copy-done.2
  205.6 0.8 copy.40
  206.4 0.0 copy-done
  206.4 0.0 copy-start.1
  206.4 0.0 copy-start.5
  206.4 0.0 copy-start.3
  206.4 0.0 copy-start.4
  206.4 1.5 copy.41
  207.9 0.0 copy-done.1
  207.9 0.8 copy.42
  208.8 0.0 copy-done.5
  208.8 0.7 copy.43
  209.4 0.0 copy-done.3
  209.4 0.7 copy.44
  210.1 0.0 copy-done.4
  210.1 0.7 copy.45
  (1 shorter events, 0.0 us)
Async XLA Ops:
  199.8 5.8 %copy-start.2 = (bf16[5,64,1024]{2,1,0:T(8,128)(2,1)S(1)}, bf16[5,64,1024]{2,1,0:T(8,128)(2,1)}, u32[]{:S(2)}) copy-start(bf16[5,64,1024]{2,1,0:T(8,128)(2,1)} %get-tuple-element.23) | copy-start | bytes 1966084
  201.6 4.8 %copy-start = (bf16[5,256,1024]{2,1,0:T(8,128)(2,1)S(1)}, bf16[5,256,1024]{2,1,0:T(8,128)(2,1)}, u32[]{:S(2)}) copy-start(bf16[5,256,1024]{2,1,0:T(8,128)(2,1)} %get-tuple-element.24) | copy-start | bytes 7864324
  206.4 1.5 copy-start.1
  206.4 2.4 %copy-start.5 = (f32[2,32,512]{2,1,0:T(8,128)S(1)}, f32[2,32,512]{2,1,0:T(8,128)}, u32[]{:S(2)}) copy-start(f32[2,32,512]{2,1,0:T(8,128)} %get-tuple-element.27) | copy-start | bytes 393220
  206.4 3.0 %copy-start.3 = (f32[2,32,1024]{2,1,0:T(8,128)S(1)}, f32[2,32,1024]{2,1,0:T(8,128)}, u32[]{:S(2)}) copy-start(f32[2,32,1024]{2,1,0:T(8,128)} %get-tuple-element.28) | copy-start | bytes 786436
  206.4 3.7 %copy-start.4 = (f32[2,16,1024]{2,1,0:T(8,128)S(1)}, f32[2,16,1024]{2,1,0:T(8,128)}, u32[]{:S(2)}) copy-start(f32[2,16,1024]{2,1,0:T(8,128)} %get-tuple-element.29) | copy-start | bytes 393220

commit v2 on v1

--- a/solution.py
+++ b/solution.py
@@ -156,26 +156,15 @@
 
 
 def add_into(target, arrived):
-    lead = target.shape[:-2]
-    count = 1
-    for size in lead:
-        count *= size
-
-    @pl.loop(0, count)
-    def _(flat):
-        index = []
-        for size in reversed(lead):
-            index.insert(0, lax.rem(flat, size))
-            flat = lax.div(flat, size)
-        index = tuple(index)
-        target[index] = (target[index].astype(F32) + arrived[index].astype(F32)).astype(target.dtype)
+    @pl.loop(0, target.shape[0])
+    def _(number):
+        target[number] = (target[number].astype(F32) + arrived[number].astype(F32)).astype(target.dtype)
 
 
 def run(table, tick):
-    for item, first, stride in table:
-        late = tick - first
-        if late >= 0 and late % stride == 0:
-            item.step(late // stride)
+    for item, ticks in table:
+        if tick in ticks:
+            item.step(ticks.index(tick))
 
 
 def matmul(left, right):
@@ -362,19 +351,21 @@
 
         return Gather(links, slots, view, order, True)
 
+    vector_gather = Gather(links, slots, lambda zi, yi, xi: packed_all.at[zi, yi, xi], xy, False)
     gathers = [
-        (Gather(links, slots, lambda zi, yi, xi: packed_all.at[zi, yi, xi], xy, False), 0, 1),
-        (halves(context_all, 0, width // 2, xy), 0, 1), (halves(context_all, width // 2, width // 2, yx), 0, 1),
-        (halves(query_all, 0, inner, xy), 1, 1), (halves(output_all, 0, width, yx), 1, 1),
+        (halves(context_all, 0, width // 2, xy), (0, 1, 2, 3, 4)),
+        (halves(context_all, width // 2, width // 2, yx), (0, 1, 2, 3, 4)),
+        (halves(query_all, 0, inner, xy), (1, 2, 3, 4, 5)), (halves(output_all, 0, width, yx), (1, 2, 3, 4, 5)),
     ]
-    for number in range(chunks):
-        window = pl.ds(number * (width // chunks), width // chunks)
-        gathers.append((Gather(links, slots, lambda zi, yi, xi, window=window: down_all.at[zi, yi, :, window],
-                               ("z", "y"), False), 2 + number, 2))
-    for number in range(chunks):
-        window = pl.ds(number * chunk, chunk)
-        gathers.append((Gather(links, slots, lambda zi, yi, xi, window=window: up_all.at[zi, yi, ALL, :, window],
-                               ("z", "y"), False), 2 + chunks + number, 2))
+    for number in range(2 * chunks):
+        window = pl.ds(number % chunks * chunk, chunk)
+        if number < chunks:
+            def view(zi, yi, xi, window=window):
+                return down_all.at[zi, yi, :, window]
+        else:
+            def view(zi, yi, xi, window=window):
+                return up_all.at[zi, yi, ALL, :, window]
+        gathers.append((Gather(links, slots, view, ("z", "y"), False), (number, number + 3, number + 5)))
     up_across = slots.move(links.device("x"), up_stage, up_all.at[z, y, x], up_all.at[z, y, 1 - x])
     gathered = len(slots.made)
     parts = [(0, 2 * latent_count), (2 * latent_count, rows - 2 * latent_count)]
@@ -384,48 +375,36 @@
     def pump(tick):
         run(gathers, tick)
 
-    for copy in staged:
+    for copy in staged + later:
         copy.wait()
+    vector_gather.step(0)
     pump(0)
+    up_across.start()
     grad_load.wait()
-    count = counts[0]
-
-    def keep(j):
-        return jnp.where(j < count, 1.0, 0.0)
-
-    for j in range(slot_count):
-        branch[pl.ds(j * latent_count, latent_count)] = (grad_in[j].astype(F32) * keep(j)).astype(BF16)
+    kept = jnp.where(lax.broadcasted_iota(jnp.int32, (rows, 1), 0) < counts[0] * latent_count, 1.0, 0.0)
+    branch[:rows] = (grad_in[...].reshape(rows, width).astype(F32) * kept).astype(BF16)
+    vector_gather.step(1)
     mask[...] = head_mask(latent_count, GROUP)
     sums[...] = jnp.zeros_like(sums)
-    for copy in later:
-        copy.wait()
-    pump(1)
-    up_across.start()
-    pump(2)
+    vector_gather.step(2)
     latents_load.wait()
     media_load.wait()
-    pump(3)
+    pump(1)
+    vector_gather.step(3)
     lane = packed_all.shape[-1]
     for zi in range(length):
         for yi in range(2):
             place = (zi * 2 + yi) * lane
             vectors[:, place:place + lane] = (packed_all[zi, yi, 0] + packed_all[zi, yi, 1]).astype(F32)[:8]
 
-    step = 32
-
     def normalise_slot(j):
-        def media_tile(at):
-            context[j, pl.ds(at, step)] = layer_norm(
-                media_in[j, pl.ds(at, step)].astype(F32), vectors[0:1], vectors[1:2]).astype(BF16)
-
-        def latent_tile(at):
-            context[j, pl.ds(patches + at, step)] = layer_norm(
-                latents_in[j, pl.ds(at, step)].astype(F32), vectors[2:3], vectors[3:4]).astype(BF16)
-
-        tiles(patches // step, step, media_tile)
-        tiles(latent_count // step, step, latent_tile)
+        context[j, :patches] = layer_norm(media_in[j].astype(F32), vectors[0:1], vectors[1:2]).astype(BF16)
+        context[j, patches:] = layer_norm(latents_in[j].astype(F32), vectors[2:3], vectors[3:4]).astype(BF16)
 
     pl.loop(0, slot_count)(normalise_slot)
+    pump(2)
+    pump(3)
+    up_across.wait()
     pump(4)
     branch_rows.send(0)
 
@@ -438,7 +417,6 @@
     latent_normed = context[:, patches:, :].reshape(rows, width)
     query[...] = (matmul(latent_normed, query_all[...].reshape(width, inner)) * scaling).astype(BF16).reshape(
         slot_count, latent_count, inner)
-    up_across.wait()
     pump(6)
 
     def attention_slot(j):
@@ -448,21 +426,17 @@
             value = matmul(probs, key_value[j, :, inner + begin:inner + begin + GROUP])
             attended[j, :, begin:begin + GROUP] = pick_heads(value, mask[...], latent_count).astype(BF16)
 
-    def feed_tile(at):
-        feed[pl.ds(at, step)] = layer_norm(after[pl.ds(at, step)], vectors[4:5], vectors[5:6]).astype(BF16)
-
     for part, (begin, size) in enumerate(parts):
         first, last = begin // latent_count, (begin + size) // latent_count
         pl.loop(first, last)(attention_slot)
         after[begin:begin + size] = latents_in[first:last].reshape(size, width).astype(F32) + matmul(
             attended[first:last].reshape(size, inner), output_all[...].reshape(inner, width))
-        pl.loop(begin // step, (begin + size) // step)(lambda n: feed_tile(pl.multiple_of(n * step, step)))
+        feed[begin:begin + size] = layer_norm(
+            after[begin:begin + size], vectors[4:5], vectors[5:6]).astype(BF16)
         feed_rows.send(part)
         pump(7 + part)
     branch_rows.near(0)
     branch_rows.forward(0)
-    pump(9)
-    branch_rows.far(0)
 
     def turn(source, target, owner):
         def body(at):
@@ -471,6 +445,8 @@
 
         tiles(width // 256, 256, body)
 
+    turn(branch, branch_t, 0)
+    branch_rows.far(0)
     tall = rows
     d_active, active, d_hidden = [pool.at[pl.ds(n * 4 * rows, 4 * rows)] for n in range(3)]
 
@@ -479,12 +455,8 @@
             branch[pl.ds(at, tall)], down_all[...].reshape(hidden, width)).astype(BF16)
 
     tiles(4, tall, d_active_tile)
-    turn(branch, branch_t, 0)
     turn(branch, branch_t, 2)
-    pump(10)
-    feed_rows.forward(0)
-    feed_rows.near(0)
-    feed_rows.near(1)
+    pump(9)
 
     def hidden_tile(at, begin):
         window = pl.ds(begin, chunk)
@@ -493,27 +465,6 @@
         active[pl.ds(at, tall), window] = value.astype(BF16)
         d_hidden[pl.ds(at, tall), window] = (d_active[pl.ds(at, tall), window].astype(F32) * slope).astype(BF16)
 
-    for c in range(chunks):
-        tiles(2, tall, lambda at, c=c: hidden_tile(at, c * chunk))
-        if c == 0:
-            feed_rows.forward(1)
-            turn(feed, feed_t, 0)
-        pump(11 + c)
-    feed_rows.far(0)
-    feed_rows.far(1)
-    for move in slots.made[:gathered]:
-        move.drain()
-    feed_rows.drain()
-    branch_rows.drain()
-    d_feed_back = Partials(links, slots, feed, d_feed_lands, rows)
-    after_back = Partials(links, slots, branch, after_lands, rows)
-    turn(feed, feed_t, 2)
-
-    def far_tile(at):
-        pl.loop(0, chunks)(lambda c: hidden_tile(pl.multiple_of(2 * rows + at, tall), pl.multiple_of(c * chunk, chunk)))
-
-    tiles(2, tall, far_tile)
-
     def d_feed_of(owner):
         return matmul_right(d_hidden[pl.ds(owner * rows, rows)], up_all[...].reshape(width, hidden))
 
@@ -523,23 +474,8 @@
     def rounded(buffer, owner, value):
         buffer[pl.ds(owner * rows, rows)] = value.astype(BF16)
 
-    rounded(feed, 3, d_feed_of(3))
-    d_feed_back.far.start()
-    totals[1] = d_feed_of(2)
-    d_feed_back.far.wait()
-
     def across_tile(back, buffer):
-        def body(at):
-            here = pl.ds(at, step)
-            buffer[pl.ds(2 * rows + at, step)] = (totals[1, here] + back.lands[0, here].astype(F32)).astype(BF16)
-
-        tiles(rows // step, step, body)
-
-    across_tile(d_feed_back, feed)
-    d_feed_back.across.start()
-    rounded(feed, 1, d_feed_of(1))
-    d_feed_back.near.start()
-    totals[0] = d_feed_of(0)
+        rounded(buffer, 2, totals[1] + back.lands[0].astype(F32))
 
     up_result, down_result, query_result, context_result, output_result = result
     reductions = []
@@ -554,9 +490,34 @@
         up_result[0, :, window] = jnp.where(x == 0, value[0], value[1])
         own_rows_send[:, window] = jnp.where(x == 0, value[1], value[0]).astype(BF16)
 
+    feed_rows.near(0)
+    feed_rows.near(1)
     for c in range(chunks):
         begin = c * chunk
         window = pl.ds(begin, chunk)
+        tiles(2, tall, lambda at, begin=begin: hidden_tile(at, begin))
+        if c == 0:
+            pump(10)
+            turn(feed, feed_t, 0)
+            feed_rows.forward(0)
+            feed_rows.forward(1)
+            feed_rows.far(0)
+            feed_rows.far(1)
+            turn(feed, feed_t, 2)
+        tiles(2, tall, lambda at, begin=begin: hidden_tile(pl.multiple_of(2 * rows + at, tall), begin))
+        if c == chunks - 1:
+            for move in slots.made[:gathered]:
+                move.drain()
+            feed_rows.drain()
+            branch_rows.drain()
+            d_feed_back = Partials(links, slots, feed, d_feed_lands, rows)
+            after_back = Partials(links, slots, branch, after_lands, rows)
+            rounded(feed, 3, d_feed_of(3))
+            d_feed_back.far.start()
+            totals[1] = d_feed_of(2)
+            d_feed_back.far.wait()
+            across_tile(d_feed_back, feed)
+            d_feed_back.across.start()
 
         def grad_tile(number, window=window, c=c):
             size = width // 2
@@ -572,7 +533,9 @@
         reductions.append((plane_reduction(
             lambda zi, yi, xi, window=window: grad_up.at[zi, yi, ALL, :, window],
             lands_b[0].at[:, :, :, window], lands_z[0].at[:, :, :, window],
-            functools.partial(keep_up, window=window)), c, 2))
+            functools.partial(keep_up, window=window)), (c, c + 2, c + 4)))
+        if c < chunks - 1:
+            pump(10 + c + (1 if c > 0 else 1))
         send_off(c)
     part_size = width // chunks
     for number in range(chunks):
@@ -583,44 +546,48 @@
 
         reductions.append((plane_reduction(
             lambda zi, yi, xi, window=window: grad_down.at[zi, yi, window],
-            lands_b[1].at[:, window], lands_z[1].at[:, window], keep_down), chunks + number, 2))
+            lands_b[1].at[:, window], lands_z[1].at[:, window], keep_down),
+            (chunks, chunks + 2 + number, chunks + 4 + number)))
+    send_off(4)
+    rounded(feed, 1, d_feed_of(1))
+    d_feed_back.near.start()
+    totals[0] = d_feed_of(0)
 
     rounded(branch, 3, after_feed_of(3))
     after_back.far.start()
-    d_feed_back.near.wait()
-    d_feed_back.across.wait()
-    send_off(4)
-
-    def fold(terms):
-        return jnp.sum(terms.reshape(-1, 8, width), axis=0)
-
-    d_feed = totals.at[0]
-    d_feed_back.far.drain()
-    d_feed_back.near.drain()
-    d_feed_back.across.drain()
-
-    def middle_slot(j):
-        def body(at):
-            own = pl.ds(pl.multiple_of(j * latent_count + at, step), step)
-            upstream = d_feed[own] + d_feed_lands[1, own].astype(F32) + d_feed_lands[2, own].astype(F32)
-            d_norm, gain_terms = layer_norm_back(after[own], vectors[4:5], upstream)
-            sums[4] = sums[4] + fold(gain_terms)
-            sums[5] = sums[5] + fold(upstream)
-            d_middle = grad_in[j, pl.ds(at, step)].astype(F32) * keep(j) + d_norm
-            d_feed[own] = d_middle
-            feed[own] = d_middle.astype(BF16)
-
-        tiles(latent_count // step, step, body)
-
-    pl.loop(0, slot_count)(middle_slot)
     totals[1] = after_feed_of(2)
     after_back.far.wait()
     across_tile(after_back, branch)
-    after_back.across.start()
+    send_off(5)
     rounded(branch, 1, after_feed_of(1))
     after_back.near.start()
+    d_feed_back.near.wait()
+    d_feed_back.across.wait()
+    after_back.across.start()
+    for move in (d_feed_back.far, d_feed_back.near, d_feed_back.across):
+        move.drain()
+
+    def fold(terms):
+        return jnp.sum(terms.reshape(-1, 8, width), axis=0)
+
+    d_feed = totals.at[0]
+    flat_grad = lambda at, size: grad_in[pl.ds(lax.div(at, latent_count), size // latent_count)].reshape(size, width)
+
+    def middle_tile(at, size=latent_count):
+        own = pl.ds(at, size)
+        upstream = d_feed[own] + d_feed_lands[1, own].astype(F32) + d_feed_lands[2, own].astype(F32)
+        d_norm, gain_terms = layer_norm_back(after[own], vectors[4:5], upstream)
+        sums[4] = sums[4] + fold(gain_terms)
+        sums[5] = sums[5] + fold(upstream)
+        row = lax.broadcasted_iota(jnp.int32, (size, 1), 0) + at
+        keep = jnp.where(row < counts[0] * latent_count, 1.0, 0.0)
+        d_middle = flat_grad(at, size).astype(F32) * keep + d_norm
+        d_feed[own] = d_middle
+        feed[own] = d_middle.astype(BF16)
+
+    tiles(slot_count, latent_count, middle_tile)
+    send_off(6)
     after[...] = after[...] + after_feed_of(0)
-    send_off(5)
 
     context_rows, output_rows = context_all.shape[-2], output_all.shape[-2]
 
@@ -655,7 +622,7 @@
             made.append((Reduce(
                 links, slots, lambda zi, yi, xi, window=window: own(zi, yi, xi, rep).at[..., window], order,
                 [lands_b[number].at[:, :, :, window], lands_a[number].at[:, :, window]],
-                lands_z[number].at[:, :, window], finish), first, 1))
+                lands_z[number].at[:, :, window], finish), (first, first + 1, first + 2, first + 3)))
         return made
 
     d_branch = feed.at[pl.ds(0, rows)]
@@ -672,7 +639,7 @@
     settle_output = to_sibling(output_own, lands_c[2])
     d_attended, d_query = upstream_rows[0], upstream_rows[1]
     d_attended[...] = matmul_right(d_branch[...], output_all[...].reshape(inner, width)).astype(BF16)
-    send_off(6)
+    send_off(7)
 
     def attention_back_slot(j):
         own = pl.ds(pl.multiple_of(j * latent_count, latent_count), latent_count)
@@ -692,10 +659,10 @@
             pool[at, begin:begin + GROUP] = matmul_left(d_scores, stacked).astype(BF16)
             pool[at, inner + begin:inner + begin + GROUP] = matmul_left(probs.astype(BF16), upstream).astype(BF16)
 
-    pl.loop(0, 2)(attention_back_slot)
-    send_off(7)
-    pl.loop(2, slot_count)(attention_back_slot)
+    pl.loop(0, 3)(attention_back_slot)
     send_off(8)
+    pl.loop(3, slot_count)(attention_back_slot)
+    send_off(9)
     block = width // length
 
     def query_grad_tile(zi):
@@ -716,9 +683,7 @@
             value = term if value is None else value + term
         up_all[zi] = value.astype(BF16).reshape(2, 2, block // 4, 2 * inner)
 
-    pl.loop(0, 2)(context_grad_tile)
-    send_off(9)
-    pl.loop(2, length)(context_grad_tile)
+    pl.loop(0, length)(context_grad_tile)
     settle_context = to_sibling(context_own, lands_c[1])
     settle_output()
     settle_query()
@@ -735,10 +700,7 @@
     after_back.across.wait()
     for move in (after_back.far, after_back.near, after_back.across):
         move.drain()
-    for j in range(slot_count):
-        own = pl.ds(j * latent_count, latent_count)
-        branch[own] = ((after[own] + after_lands[1, own].astype(F32) + after_lands[2, own].astype(F32))
-                       * keep(j)).astype(BF16)
+    branch[:rows] = ((after[...] + after_lands[1].astype(F32) + after_lands[2].astype(F32)) * kept).astype(BF16)
     written = [locals_.copy(branch.at[pl.ds(j * latent_count, latent_count)], latents_out.at[j])
                for j in range(slot_count)]
 
@@ -750,25 +712,20 @@
         context_up[...] = matmul_right(pool[at], context_all[...].reshape(width, 2 * inner))
         context_up[patches:] = context_up[patches:] + matmul_right(d_query[own], query_all[...].reshape(width, inner))
 
-        def media_tile(at):
-            own = pl.ds(at, step)
-            upstream = context_up[own]
-            value, gain_terms = layer_norm_back(media_in[j, own].astype(F32), vectors[0:1], upstream)
+        def media_tile(at, size=patches // 2):
+            tile = pl.ds(at, size)
+            upstream = context_up[tile]
+            value, gain_terms = layer_norm_back(media_in[j, tile].astype(F32), vectors[0:1], upstream)
             sums[0] = sums[0] + fold(gain_terms)
             sums[1] = sums[1] + fold(upstream)
-            media_in[j, own] = value.astype(BF16)
-
-        def latent_tile(at):
-            own = pl.ds(at, step)
-            upstream = context_up[pl.ds(patches + at, step)]
-            value, gain_terms = layer_norm_back(latents_in[j, own].astype(F32), vectors[2:3], upstream)
-            sums[2] = sums[2] + fold(gain_terms)
-            sums[3] = sums[3] + fold(upstream)
-            d_middle = d_feed[pl.ds(pl.multiple_of(j * latent_count + at, step), step)]
-            latents_in[j, own] = (d_middle + value).astype(BF16)
-
-        tiles(patches // step, step, media_tile)
-        tiles(latent_count // step, step, latent_tile)
+            media_in[j, tile] = value.astype(BF16)
+
+        tiles(2, patches // 2, media_tile)
+        upstream = context_up[patches:]
+        value, gain_terms = layer_norm_back(latents_in[j].astype(F32), vectors[2:3], upstream)
+        sums[2] = sums[2] + fold(gain_terms)
+        sums[3] = sums[3] + fold(upstream)
+        latents_in[j] = (d_feed[own] + value).astype(BF16)
 
     pl.loop(0, 2)(input_slot)
     send_off(12)

time: 211 us -> 195 us (0.924)
  Pallas kernels: 194 us -> 178 us
    pallas_call x1, Pallas kernels: 194 us -> 178 us  [layer(): pl.pallas_call(functools.partial(layer_kernel, length, HEAD_DIM ** (-0.5)...]
where the time goes in v2:
time: 195 us
  Pallas kernels  178 us (91%)
  local copies, waits for them, and re-layouts  12.7 us (7%)
  other arithmetic  2.4 us (1%)
    pallas_call x1, Pallas kernels, layer(): pl.pallas_call(functools.partial(layer_kernel, length, HEAD_DIM ** (-0.5)...  178 us
    unnamed x19, local copies, waits for them, and re-layouts  5.4 us

profile of v2, /device:TPU:0, one launch (start us, length us, event | category | flops | bytes accessed | tf_op | source)
XLA Modules:
  0.0 194.5 jit_solution(1150687998438681083)
XLA Ops:
  0.7 0.8 stack.27
  1.4 0.7 fusion.2.packed
  2.7 178.0 %resampler_layer.1 = (bf16[5,64,1024]{2,1,0:T(8,128)(2,1)}, bf16[5,256,1024]{2,1,0:T(8,128)(2,1)}, bf16[5,64,1024]{2,1,0:T(8,128)(2,1)}, f32[8,1024]{1,0:T(8,128...) custom-call(s32[1]{0:T(128)S(6)} %copy.39.counts, ...), custom_call_target="tpu_custom_call" | custom-call | tf_op jit(solution)/shard_map/resampler_layer/pallas_call | solution.py:834
  180.8 1.7 reverse_select_fusion
  182.5 0.2 copy.32
  182.7 0.8 copy.30
  183.5 0.0 copy-start.2
  183.6 1.8 reshape.50
  185.4 0.0 copy-start
  185.4 0.9 constant_dynamic-slice_fusion
  186.3 0.5 slice_bitcast_fusion
  186.8 2.5 %copy.31 = f32[2,128,1024]{2,1,0:T(8,128)} copy(f32[2,128,1024]{1,2,0:T(8,128)} %bitcast.40) | data formatting | bytes 2097152 | tf_op jit(solution)/shard_map/transpose | solution.py:1032
  189.3 0.0 copy-done.2
  189.3 0.8 copy.40
  190.2 0.0 copy-done
  190.2 0.0 copy-start.1
  190.2 0.0 copy-start.5
  190.2 0.0 copy-start.3
  190.2 0.0 copy-start.4
  190.2 1.5 copy.41
  191.7 0.0 copy-done.1
  191.7 0.8 copy.42
  192.5 0.0 copy-done.5
  192.5 0.7 copy.43
  193.2 0.0 copy-done.3
  193.2 0.7 copy.44
  193.9 0.0 copy-done.4
  193.9 0.7 copy.45
  (1 shorter events, 0.0 us)
Async XLA Ops:
  183.5 5.8 %copy-start.2 = (bf16[5,64,1024]{2,1,0:T(8,128)(2,1)S(1)}, bf16[5,64,1024]{2,1,0:T(8,128)(2,1)}, u32[]{:S(2)}) copy-start(bf16[5,64,1024]{2,1,0:T(8,128)(2,1)} %get-tuple-element.23) | copy-start | bytes 1966084
  185.4 4.8 %copy-start = (bf16[5,256,1024]{2,1,0:T(8,128)(2,1)S(1)}, bf16[5,256,1024]{2,1,0:T(8,128)(2,1)}, u32[]{:S(2)}) copy-start(bf16[5,256,1024]{2,1,0:T(8,128)(2,1)} %get-tuple-element.24) | copy-start | bytes 7864324
  190.2 1.5 copy-start.1
  190.2 2.4 %copy-start.5 = (f32[2,32,512]{2,1,0:T(8,128)S(1)}, f32[2,32,512]{2,1,0:T(8,128)}, u32[]{:S(2)}) copy-start(f32[2,32,512]{2,1,0:T(8,128)} %get-tuple-element.27) | copy-start | bytes 393220
  190.2 3.0 %copy-start.3 = (f32[2,32,1024]{2,1,0:T(8,128)S(1)}, f32[2,32,1024]{2,1,0:T(8,128)}, u32[]{:S(2)}) copy-start(f32[2,32,1024]{2,1,0:T(8,128)} %get-tuple-element.28) | copy-start | bytes 786436
  190.2 3.7 %copy-start.4 = (f32[2,16,1024]{2,1,0:T(8,128)S(1)}, f32[2,16,1024]{2,1,0:T(8,128)}, u32[]{:S(2)}) copy-start(f32[2,16,1024]{2,1,0:T(8,128)} %get-tuple-element.29) | copy-start | bytes 393220

commit v3 on v2

--- a/solution.py
+++ b/solution.py
@@ -48,44 +48,63 @@
 
 
 class Move:
-    def __init__(self, send, recv, slot, device, source, target, landing):
-        self.out = pltpu.make_async_remote_copy(
-            src_ref=source, dst_ref=target, send_sem=send.at[slot], recv_sem=recv.at[slot],
-            device_id=device, device_id_type=MESH)
+    def __init__(self, slots, copies, landing):
+        send, recv = slots.send.at[slots.group], slots.recv.at[slots.made]
+        slots.made += 1
+        self.slots, self.group, self.copies = slots, slots.group, [
+            pltpu.make_async_remote_copy(
+                src_ref=source, dst_ref=target, send_sem=send, recv_sem=recv,
+                device_id=device, device_id_type=MESH)
+            for device, source, target in copies]
+        self.bytes = 0
+        for _, source, _ in copies:
+            size = jnp.dtype(source.dtype).itemsize
+            for extent in source.shape:
+                size *= extent
+            self.bytes += size
         self.into = pltpu.make_async_remote_copy(
-            src_ref=landing, dst_ref=landing, send_sem=send.at[slot], recv_sem=recv.at[slot],
-            device_id=device, device_id_type=MESH)
+            src_ref=landing, dst_ref=landing, send_sem=send, recv_sem=recv,
+            device_id=copies[0][0], device_id_type=MESH)
 
     def start(self):
-        self.out.start()
+        for copy in self.copies:
+            copy.start()
+        self.slots.sent[self.group] += self.bytes
 
     def wait(self):
         self.into.wait_recv()
 
-    drained = False
-
-    def drain(self):
-        self.drained = True
-        self.out.wait_send()
-
 
 class Slots:
-    def __init__(self, send, recv):
-        self.send, self.recv, self.made = send, recv, []
-
-    def move(self, *args):
-        self.made.append(Move(self.send, self.recv, len(self.made), *args))
-        return self.made[-1]
+    def __init__(self, send, recv, ruler):
+        self.send, self.recv, self.ruler, self.made, self.group = send, recv, ruler, 0, 0
+        self.sent = [0] * send.shape[0]
+
+    def move(self, device, source, target, landing):
+        return Move(self, [(device, source, target)], landing)
+
+    def drain(self, group, ruler=None):
+        ruler = self.ruler if ruler is None else ruler
+        row = ruler.shape[-1] * jnp.dtype(ruler.dtype).itemsize
+        rows, rest = divmod(self.sent[group], row)
+        assert rest == 0 and rows % 16 == 0 and rows <= ruler.shape[0]
+        whole = ruler.at[pl.ds(0, rows)]
+        pltpu.make_async_copy(whole, whole, self.send.at[group]).wait()
 
 
 class Locals:
     def __init__(self, semaphores):
-        self.semaphores, self.made = semaphores, []
+        self.semaphores, self.made = semaphores, 0
 
     def copy(self, source, target):
-        self.made.append(pltpu.make_async_copy(source, target, self.semaphores.at[len(self.made)]))
-        self.made[-1].start()
-        return self.made[-1]
+        return self.fill([(source, target)], target)
+
+    def fill(self, copies, whole):
+        semaphore = self.semaphores.at[self.made]
+        self.made += 1
+        for source, target in copies:
+            pltpu.make_async_copy(source, target, semaphore).start()
+        return pltpu.make_async_copy(whole, whole, semaphore)
 
 
 class Gather:
@@ -95,27 +114,25 @@
         for axis in axes:
             mine = view(here["z"], here["y"], here["x"])
             if axis == "z":
-                self.moves.append([
-                    slots.move(links.device("z", way), mine, mine, view(links.along(-way), here["y"], here["x"]))
-                    for way in range(1, links.length)])
+                self.moves.append(Move(
+                    slots, [(links.device("z", way), mine, mine) for way in range(1, links.length)],
+                    view(pl.ds(0, links.length - 1), here["y"], here["x"])))
             else:
                 other = dict(here)
                 other[axis] = 1 - here[axis]
-                self.moves.append([
-                    slots.move(links.device(axis), mine, mine, view(other["z"], other["y"], other["x"]))])
+                self.moves.append(
+                    slots.move(links.device(axis), mine, mine, view(other["z"], other["y"], other["x"])))
             here[axis] = ALL
         if halved:
             mine = view(ALL, ALL, ALL)
-            self.moves.append([
-                slots.move(links.device("core"), mine, mine, view(ALL, ALL, ALL, 1 - links.rep))])
+            self.moves.append(
+                slots.move(links.device("core"), mine, mine, view(ALL, ALL, ALL, 1 - links.rep)))
 
     def step(self, number):
         if 0 < number <= len(self.moves):
-            for move in self.moves[number - 1]:
-                move.wait()
+            self.moves[number - 1].wait()
         if 0 <= number < len(self.moves):
-            for move in self.moves[number]:
-                move.start()
+            self.moves[number].start()
 
 
 class Reduce:
@@ -128,25 +145,22 @@
             away, home = dict(here), dict(here)
             place = {"y": y, "x": x}[axis]
             away[axis], home[axis] = 1 - place, place
-            self.moves.append([slots.move(
-                links.device(axis), own(away["z"], away["y"], away["x"]), land, land)])
+            self.moves.append(slots.move(
+                links.device(axis), own(away["z"], away["y"], away["x"]), land, land))
             here = home
             self.adds.append(functools.partial(add_into, own(home["z"], home["y"], home["x"]), land))
-        self.moves.append([
-            slots.move(links.device("z", way), own(links.along(way), here["y"], here["x"]), lands_z.at[way - 1],
-                       lands_z.at[way - 1])
-            for way in range(1, links.length)])
+        self.moves.append(Move(
+            slots, [(links.device("z", way), own(links.along(way), here["y"], here["x"]), lands_z.at[way - 1])
+                    for way in range(1, links.length)], lands_z))
         self.mine = own(z, here["y"], here["x"])
         self.adds.append(self.end)
 
     def step(self, number):
         if 0 < number <= len(self.moves):
-            for move in self.moves[number - 1]:
-                move.wait()
+            self.moves[number - 1].wait()
             self.adds[number - 1]()
         if 0 <= number < len(self.moves):
-            for move in self.moves[number]:
-                move.start()
+            self.moves[number].start()
 
     def end(self):
         total = self.mine[...].astype(F32)
@@ -246,22 +260,20 @@
 class VectorSum:
     def __init__(self, links, slots, total, stage, lands):
         self.total, self.stage, self.lands, self.length = total, stage, lands, links.length
-        self.moves = [[slots.move(links.device(axis), stage.at[number], lands.at[number], lands.at[number])]
+        self.moves = [slots.move(links.device(axis), stage.at[number], lands.at[number], lands.at[number])
                       for number, axis in enumerate(("core", "x", "y"))]
-        self.moves.append([
-            slots.move(links.device("z", way), stage.at[3], lands.at[2 + way], lands.at[2 + way])
-            for way in range(1, links.length)])
+        self.moves.append(Move(
+            slots, [(links.device("z", way), stage.at[3], lands.at[2 + way]) for way in range(1, links.length)],
+            lands.at[pl.ds(3, links.length - 1)]))
 
     def step(self, number):
         if 0 < number <= 4:
-            for move in self.moves[number - 1]:
-                move.wait()
+            self.moves[number - 1].wait()
             for land in ([number - 1] if number < 4 else range(3, 2 + self.length)):
                 self.total[...] = self.total[...] + self.lands[land]
         if number < 4:
             self.stage[number] = self.total[...]
-            for move in self.moves[number]:
-                move.start()
+            self.moves[number].start()
 
 
 class Rows:
@@ -289,10 +301,6 @@
 
     def far(self, part):
         self.passed[part].wait()
-
-    def drain(self):
-        for move in [m for pair in self.moves for m in pair] + self.passed:
-            move.drain()
 
 
 class Partials:
@@ -315,7 +323,7 @@
                  own_rows_send, own_rows_land, lands_c, lands_b, lands_a, lands_z, result, send, recv, local):
     links = Links(length)
     z, y, x, rep = links.z, links.y, links.x, links.rep
-    slots, locals_ = Slots(send, recv), Locals(local)
+    slots, locals_ = Slots(send, recv, pool), Locals(local)
     slot_count, patches, width = media.shape
     latent_count = latents.shape[1]
     key_count = patches + latent_count
@@ -334,12 +342,13 @@
     for shard, whole in ((context_shard, context_all), (query_shard, query_all), (output_shard, output_all)):
         half = whole.shape[-2]
         staged.append(locals_.copy(shard.at[pl.ds(pl.multiple_of(rep * half, 16), half)], whole.at[z, y, x, rep]))
-    later = []
-    for number in range(hidden // unit):
-        window = pl.ds(number * unit, unit)
-        later.append(locals_.copy(up_shard.at[:, unit_columns(1 - x, number)], up_stage.at[:, window]))
-        later.append(locals_.copy(up_shard.at[:, unit_columns(x, number)], up_all.at[z, y, x, :, window]))
-    later.append(locals_.copy(down_shard.at[pl.ds(pl.multiple_of(rep * unit, 16), unit)], down_all.at[z, y]))
+    units = range(hidden // unit)
+    staged.append(locals_.fill(
+        [(up_shard.at[:, unit_columns(1 - x, n)], up_stage.at[:, pl.ds(n * unit, unit)]) for n in units], up_stage))
+    staged.append(locals_.fill(
+        [(up_shard.at[:, unit_columns(x, n)], up_all.at[z, y, x, :, pl.ds(n * unit, unit)]) for n in units],
+        up_all.at[z, y, x]))
+    staged.append(locals_.copy(down_shard.at[pl.ds(pl.multiple_of(rep * unit, 16), unit)], down_all.at[z, y]))
     grad_load = locals_.copy(grad_out, grad_in)
     latents_load = locals_.copy(latents, latents_in)
     media_load = locals_.copy(media, media_in)
@@ -351,12 +360,15 @@
 
         return Gather(links, slots, view, order, True)
 
+    slots.group = 0
     vector_gather = Gather(links, slots, lambda zi, yi, xi: packed_all.at[zi, yi, xi], xy, False)
+    slots.group = 1
     gathers = [
         (halves(context_all, 0, width // 2, xy), (0, 1, 2, 3, 4)),
         (halves(context_all, width // 2, width // 2, yx), (0, 1, 2, 3, 4)),
-        (halves(query_all, 0, inner, xy), (1, 2, 3, 4, 5)), (halves(output_all, 0, width, yx), (1, 2, 3, 4, 5)),
+        (halves(query_all, 0, inner, yx), (0, 2, 3, 4, 5)), (halves(output_all, 0, width, yx), (0, 2, 3, 4, 5)),
     ]
+    slots.group = 2
     for number in range(2 * chunks):
         window = pl.ds(number % chunks * chunk, chunk)
         if number < chunks:
@@ -365,9 +377,13 @@
         else:
             def view(zi, yi, xi, window=window):
                 return up_all.at[zi, yi, ALL, :, window]
-        gathers.append((Gather(links, slots, view, ("z", "y"), False), (number, number + 3, number + 5)))
+        if number == chunks - 1:
+            gathers.append((Gather(links, slots, view, ("y", "z"), False), (0, 2, 7)))
+        else:
+            ticks = (max(number - 1, 0), number + 2, number + 4)
+            gathers.append((Gather(links, slots, view, ("z", "y"), False), ticks))
     up_across = slots.move(links.device("x"), up_stage, up_all.at[z, y, x], up_all.at[z, y, 1 - x])
-    gathered = len(slots.made)
+    slots.group = 3
     parts = [(0, 2 * latent_count), (2 * latent_count, rows - 2 * latent_count)]
     branch_rows = Rows(links, slots, branch, rows, [(0, rows)])
     feed_rows = Rows(links, slots, feed, rows, parts)
@@ -375,7 +391,7 @@
     def pump(tick):
         run(gathers, tick)
 
-    for copy in staged + later:
+    for copy in staged:
         copy.wait()
     vector_gather.step(0)
     pump(0)
@@ -403,8 +419,8 @@
 
     pl.loop(0, slot_count)(normalise_slot)
     pump(2)
+    up_across.wait()
     pump(3)
-    up_across.wait()
     pump(4)
     branch_rows.send(0)
 
@@ -435,6 +451,7 @@
             after[begin:begin + size], vectors[4:5], vectors[5:6]).astype(BF16)
         feed_rows.send(part)
         pump(7 + part)
+    slots.drain(0, grad_down.at[0, 0])
     branch_rows.near(0)
     branch_rows.forward(0)
 
@@ -456,7 +473,6 @@
 
     tiles(4, tall, d_active_tile)
     turn(branch, branch_t, 2)
-    pump(9)
 
     def hidden_tile(at, begin):
         window = pl.ds(begin, chunk)
@@ -492,12 +508,13 @@
 
     feed_rows.near(0)
     feed_rows.near(1)
+    slots.group = 6
     for c in range(chunks):
         begin = c * chunk
         window = pl.ds(begin, chunk)
         tiles(2, tall, lambda at, begin=begin: hidden_tile(at, begin))
         if c == 0:
-            pump(10)
+            pump(9)
             turn(feed, feed_t, 0)
             feed_rows.forward(0)
             feed_rows.forward(1)
@@ -506,12 +523,13 @@
             turn(feed, feed_t, 2)
         tiles(2, tall, lambda at, begin=begin: hidden_tile(pl.multiple_of(2 * rows + at, tall), begin))
         if c == chunks - 1:
-            for move in slots.made[:gathered]:
-                move.drain()
-            feed_rows.drain()
-            branch_rows.drain()
+            for group in range(1, 4):
+                slots.drain(group)
+            slots.group = 4
             d_feed_back = Partials(links, slots, feed, d_feed_lands, rows)
+            slots.group = 5
             after_back = Partials(links, slots, branch, after_lands, rows)
+            slots.group = 6
             rounded(feed, 3, d_feed_of(3))
             d_feed_back.far.start()
             totals[1] = d_feed_of(2)
@@ -534,15 +552,17 @@
             lambda zi, yi, xi, window=window: grad_up.at[zi, yi, ALL, :, window],
             lands_b[0].at[:, :, :, window], lands_z[0].at[:, :, :, window],
             functools.partial(keep_up, window=window)), (c, c + 2, c + 4)))
-        if c < chunks - 1:
-            pump(10 + c + (1 if c > 0 else 1))
+        if c == 0:
+            pump(10)
+        if c == chunks - 2:
+            pump(11)
         send_off(c)
     part_size = width // chunks
     for number in range(chunks):
         window = pl.ds(number * part_size, part_size)
 
         def keep_down(value, window=window):
-            down_result[window] = value
+            down_result[:, window] = value.T
 
         reductions.append((plane_reduction(
             lambda zi, yi, xi, window=window: grad_down.at[zi, yi, window],
@@ -564,8 +584,7 @@
     d_feed_back.near.wait()
     d_feed_back.across.wait()
     after_back.across.start()
-    for move in (d_feed_back.far, d_feed_back.near, d_feed_back.across):
-        move.drain()
+    slots.drain(4)
 
     def fold(terms):
         return jnp.sum(terms.reshape(-1, 8, width), axis=0)
@@ -610,11 +629,10 @@
 
         return settle
 
-    def halved_reduction(own, number, target, first):
+    def halved_reduction(own, number, target, begin, size, *ticks):
         made = []
-        size = target.shape[-1] // 2
         for which, order in enumerate((("y", "x"), ("x", "y"))):
-            window = pl.ds(which * size, size)
+            window = pl.ds(begin + which * (size // 2), size // 2)
 
             def finish(value, window=window):
                 target[:, window] = value
@@ -622,7 +640,7 @@
             made.append((Reduce(
                 links, slots, lambda zi, yi, xi, window=window: own(zi, yi, xi, rep).at[..., window], order,
                 [lands_b[number].at[:, :, :, window], lands_a[number].at[:, :, window]],
-                lands_z[number].at[:, :, window], finish), (first, first + 1, first + 2, first + 3)))
+                lands_z[number].at[:, :, window], finish), ticks))
         return made
 
     d_branch = feed.at[pl.ds(0, rows)]
@@ -660,6 +678,8 @@
             pool[at, inner + begin:inner + begin + GROUP] = matmul_left(probs.astype(BF16), upstream).astype(BF16)
 
     pl.loop(0, 3)(attention_back_slot)
+    settle_output()
+    reductions.extend(halved_reduction(output_own, 4, output_result, 0, width, 8, 9, 10, 11))
     send_off(8)
     pl.loop(3, slot_count)(attention_back_slot)
     send_off(9)
@@ -685,24 +705,21 @@
 
     pl.loop(0, length)(context_grad_tile)
     settle_context = to_sibling(context_own, lands_c[1])
-    settle_output()
     settle_query()
-    first = 2 * chunks + 2
-    reductions.extend(halved_reduction(output_own, 4, output_result, first))
-    reductions.extend(halved_reduction(query_own, 2, query_result, first))
+    reductions.extend(halved_reduction(query_own, 2, query_result, 0, inner, 10, 11, 12, 13))
+    settle_context()
+    reductions.extend(halved_reduction(context_own, 3, context_result, 0, inner, 10, 11, 12, 13))
+    reductions.extend(halved_reduction(context_own, 3, context_result, inner, inner, 10, 12, 13, 14))
     send_off(10)
-    settle_context()
-    reductions.extend(halved_reduction(context_own, 3, context_result, first + 1))
-    send_off(11)
+    slots.group = 7
     own_rows_move = slots.move(links.device("x"), own_rows_send, own_rows_land, own_rows_land)
     own_rows_move.start()
     after_back.near.wait()
     after_back.across.wait()
-    for move in (after_back.far, after_back.near, after_back.across):
-        move.drain()
+    slots.drain(5)
     branch[:rows] = ((after[...] + after_lands[1].astype(F32) + after_lands[2].astype(F32)) * kept).astype(BF16)
-    written = [locals_.copy(branch.at[pl.ds(j * latent_count, latent_count)], latents_out.at[j])
-               for j in range(slot_count)]
+    written = [locals_.fill(
+        [(branch.at[pl.ds(j * latent_count, latent_count)], latents_out.at[j]) for j in range(slot_count)], latents_out)]
 
     context_up = totals.at[1]
 
@@ -728,34 +745,41 @@
         latents_in[j] = (d_feed[own] + value).astype(BF16)
 
     pl.loop(0, 2)(input_slot)
+    send_off(11)
+    pl.loop(2, 3)(input_slot)
     send_off(12)
     own_rows_move.wait()
     up_result[1] = own_rows_land[...].astype(F32)
-    pl.loop(2, 3)(input_slot)
-    send_off(13)
+
+    def hand_over(numbers):
+        for number in numbers:
+            value, out = result[number], grads_out[number]
+            written.append(locals_.copy(value, out.at[rep]))
+            written.append(slots.move(links.device("core"), value, out.at[rep], out.at[1 - rep]))
+            written[-1].start()
+
+    hand_over((0, 1))
     pl.loop(3, slot_count)(input_slot)
-    send_off(14)
     written.append(locals_.copy(media_in, media_grad_out))
     written.append(locals_.copy(latents_in, latents_grad_out))
-    total[...] = jnp.zeros_like(total)
     for number in range(6):
         total[number:number + 1] = jnp.sum(sums[number], axis=0, keepdims=True)
+    total[6:] = jnp.zeros_like(total[6:])
     vector_sum = VectorSum(links, slots, total, total_stage, total_lands)
     vector_sum.step(0)
-    send_off(15)
-    for value, out in zip(result, grads_out):
-        written.append(locals_.copy(value, out.at[rep]))
-        move = slots.move(links.device("core"), value, out.at[rep], out.at[1 - rep])
-        move.start()
-        written.append(move)
-    for number in range(1, 5):
-        vector_sum.step(number)
+    send_off(13)
+    vector_sum.step(1)
+    hand_over((2, 4))
+    vector_sum.step(2)
+    send_off(14)
+    hand_over((3,))
+    vector_sum.step(3)
+    vector_sum.step(4)
     sums_out[...] = total[...]
     for copy in written:
         copy.wait()
-    for move in slots.made:
-        if not move.drained:
-            move.drain()
+    slots.drain(6)
+    slots.drain(7)
 
 
 def layer(length, counts, media, latents, grad_out, packed, shards):
@@ -775,7 +799,7 @@
     up_shape = blocks + (up_shard.shape[0], hidden)
     down_shape = (length, 2, unit, width)
     halves = [halved(s)[4:] for s in shards[:3]]
-    results = [(2,) + up_shape[3:], (width, unit)] + halves
+    results = [(2,) + up_shape[3:], (unit, width)] + halves
     anywhere = pl.BlockSpec(memory_space=pl.ANY)
     vmem = pl.BlockSpec(memory_space=pltpu.VMEM)
     sums_shape = (8, width)
@@ -823,9 +847,9 @@
         [pltpu.VMEM((length - 1, 2) + up_shape[3:], BF16), pltpu.VMEM((length - 1, width, unit), BF16)]
         + [pltpu.VMEM((length - 1,) + h, BF16) for h in halves],
         [pltpu.VMEM(r, F32) for r in results],
-        pltpu.SemaphoreType.DMA((200,)),
-        pltpu.SemaphoreType.DMA((200,)),
-        pltpu.SemaphoreType.DMA((64,)),
+        pltpu.SemaphoreType.DMA((8,)),
+        pltpu.SemaphoreType.DMA((112,)),
+        pltpu.SemaphoreType.DMA((24,)),
     ]
     out_shape = (
         jax.ShapeDtypeStruct(latents.shape, BF16), jax.ShapeDtypeStruct(media.shape, BF16),
@@ -1026,10 +1050,10 @@
         chips // 4, image_counts, media[0], latents[0], grad_out[0], packed, weight_shards)
     sums = [s.reshape(-1, s.shape[-1]) for s in summed[2:]]
     rows, hidden = summed[0].shape[2:]
-    unit = summed[1].shape[-1]
+    unit = summed[1].shape[1]
     planes = jnp.where(lax.rem(lax.axis_index("dp"), 2) == 0, summed[0], summed[0][:, ::-1])
     sums.append(planes.reshape(2, 2, rows, hidden // unit, unit).transpose(2, 3, 1, 0, 4).reshape(rows, 4 * hidden))
-    sums.append(summed[1].transpose(0, 2, 1).reshape(2 * unit, -1))
+    sums.append(summed[1].reshape(-1, summed[1].shape[-1]))
     width = parameters[0].shape[0]
     mine = lax.dynamic_slice(vector_sums, (0, lax.axis_index("dp") * width), (6, width))
     return (latents_out[None], grad_media[None], grad_latents[None]) + tuple(mine) + tuple(sums)

time: 195 us -> 194 us (level)
  Pallas kernels: 178 us -> 176 us
    unnamed x19 -> x20, local copies, waits for them, and re-layouts: 5.4 us -> 8.65 us
    transpose x1 -> x0, local copies, waits for them, and re-layouts: 2.53 us -> none  [body(): sums.append(summed[1].transpose(0, 2, 1).reshape(2 * unit, -1))]
where the time goes in v3:
time: 194 us; the launch traced here: 193 us
  Pallas kernels  176 us (91%)
  local copies, waits for them, and re-layouts  13.3 us (7%)
  other arithmetic  2.4 us (1%)
    pallas_call x1, Pallas kernels, layer(): pl.pallas_call(functools.partial(layer_kernel, length, HEAD_DIM ** (-0.5)...  176 us
    unnamed x20, local copies, waits for them, and re-layouts  8.65 us

profile of v3, /device:TPU:0, one launch (start us, length us, event | category | flops | bytes accessed | tf_op | source)
XLA Modules:
  0.0 193.5 jit_solution(5210140346758518884)
XLA Ops:
  0.7 0.8 stack.27
  1.4 0.7 fusion.2.packed
  2.7 176.4 %resampler_layer.1 = (bf16[5,64,1024]{2,1,0:T(8,128)(2,1)}, bf16[5,256,1024]{2,1,0:T(8,128)(2,1)}, bf16[5,64,1024]{2,1,0:T(8,128)(2,1)}, f32[8,1024]{1,0:T(8,128...) custom-call(s32[1]{0:T(128)S(6)} %copy.38.counts, ...), custom_call_target="tpu_custom_call" | custom-call | tf_op jit(solution)/shard_map/resampler_layer/pallas_call | solution.py:858
  179.1 1.7 reverse_select_fusion
  180.9 0.2 copy.30
  181.1 0.0 copy-start.2
  181.1 0.8 copy.29
  181.9 1.8 reshape.50
  183.7 0.7 constant_dynamic-slice_fusion
  184.5 0.5 slice_bitcast_fusion
  185.0 0.0 copy-done.2
  185.0 0.8 copy.39
  185.8 0.0 copy-start.1
  185.8 0.0 copy-start.5
  185.8 0.0 copy-start.3
  185.8 0.0 copy-start.4
  185.8 0.0 copy-start
  185.9 3.8 %copy.40 = bf16[1,5,256,1024]{3,2,1,0:T(8,128)(2,1)} copy(bf16[1,5,256,1024]{3,2,1,0:T(8,128)(2,1)} %bitcast.38) | data formatting | bytes 5242880
  189.6 0.0 copy-done.1
  189.6 0.8 copy.41
  190.5 0.0 copy-done.5
  190.5 0.7 copy.42
  191.1 0.0 copy-done.3
  191.1 0.7 copy.43
  191.8 0.0 copy-done.4
  191.8 0.7 copy.44
  192.5 0.0 copy-done
  192.5 1.0 copy.45
  (1 shorter events, 0.0 us)
Async XLA Ops:
  181.1 3.9 %copy-start.2 = (bf16[5,64,1024]{2,1,0:T(8,128)(2,1)S(1)}, bf16[5,64,1024]{2,1,0:T(8,128)(2,1)}, u32[]{:S(2)}) copy-start(bf16[5,64,1024]{2,1,0:T(8,128)(2,1)} %get-tuple-element.23) | copy-start | bytes 1966084
  185.8 3.8 %copy-start.1 = (bf16[5,64,1024]{2,1,0:T(8,128)(2,1)S(1)}, bf16[5,64,1024]{2,1,0:T(8,128)(2,1)}, u32[]{:S(2)}) copy-start(bf16[5,64,1024]{2,1,0:T(8,128)(2,1)} %get-tuple-element.25) | copy-start | bytes 1966084
  185.8 4.6 %copy-start.5 = (f32[2,32,512]{2,1,0:T(8,128)S(1)}, f32[2,32,512]{2,1,0:T(8,128)}, u32[]{:S(2)}) copy-start(f32[2,32,512]{2,1,0:T(8,128)} %get-tuple-element.27) | copy-start | bytes 393220
  185.8 5.3 %copy-start.3 = (f32[2,32,1024]{2,1,0:T(8,128)S(1)}, f32[2,32,1024]{2,1,0:T(8,128)}, u32[]{:S(2)}) copy-start(f32[2,32,1024]{2,1,0:T(8,128)} %get-tuple-element.28) | copy-start | bytes 786436
  185.8 6.0 %copy-start.4 = (f32[2,16,1024]{2,1,0:T(8,128)S(1)}, f32[2,16,1024]{2,1,0:T(8,128)}, u32[]{:S(2)}) copy-start(f32[2,16,1024]{2,1,0:T(8,128)} %get-tuple-element.29) | copy-start | bytes 393220
  185.8 6.6 %copy-start = (f32[2,128,1024]{2,1,0:T(8,128)S(1)}, f32[2,128,1024]{2,1,0:T(8,128)}, u32[]{:S(2)}) copy-start(f32[2,128,1024]{2,1,0:T(8,128)} %get-tuple-element.31) | copy-start | bytes 3145732

commit v4 on v3

--- a/solution.py
+++ b/solution.py
@@ -377,11 +377,8 @@
         else:
             def view(zi, yi, xi, window=window):
                 return up_all.at[zi, yi, ALL, :, window]
-        if number == chunks - 1:
-            gathers.append((Gather(links, slots, view, ("y", "z"), False), (0, 2, 7)))
-        else:
-            ticks = (max(number - 1, 0), number + 2, number + 4)
-            gathers.append((Gather(links, slots, view, ("z", "y"), False), ticks))
+        ticks = (max(number - 1, 0), number + 2, number + 4)
+        gathers.append((Gather(links, slots, view, ("z", "y"), False), ticks))
     up_across = slots.move(links.device("x"), up_stage, up_all.at[z, y, x], up_all.at[z, y, 1 - x])
     slots.group = 3
     parts = [(0, 2 * latent_count), (2 * latent_count, rows - 2 * latent_count)]
@@ -551,7 +548,7 @@
         reductions.append((plane_reduction(
             lambda zi, yi, xi, window=window: grad_up.at[zi, yi, ALL, :, window],
             lands_b[0].at[:, :, :, window], lands_z[0].at[:, :, :, window],
-            functools.partial(keep_up, window=window)), (c, c + 2, c + 4)))
+            functools.partial(keep_up, window=window)), (c, c + 3, c + 5)))
         if c == 0:
             pump(10)
         if c == chunks - 2:
@@ -567,7 +564,7 @@
         reductions.append((plane_reduction(
             lambda zi, yi, xi, window=window: grad_down.at[zi, yi, window],
             lands_b[1].at[:, window], lands_z[1].at[:, window], keep_down),
-            (chunks, chunks + 2 + number, chunks + 4 + number)))
+            (chunks, chunks + 3 + number, chunks + 5 + number)))
     send_off(4)
     rounded(feed, 1, d_feed_of(1))
     d_feed_back.near.start()
@@ -581,6 +578,7 @@
     send_off(5)
     rounded(branch, 1, after_feed_of(1))
     after_back.near.start()
+    totals[1] = after_feed_of(0)
     d_feed_back.near.wait()
     d_feed_back.across.wait()
     after_back.across.start()
@@ -606,7 +604,6 @@
 
     tiles(slot_count, latent_count, middle_tile)
     send_off(6)
-    after[...] = after[...] + after_feed_of(0)
 
     context_rows, output_rows = context_all.shape[-2], output_all.shape[-2]
 
@@ -653,8 +650,6 @@
         grad_output[pl.ds(number * (length // 2), length // 2)] = value.reshape(
             length // 2, 2, 2, 2, output_rows, width)
 
-    pl.loop(0, 2)(output_grad_tile)
-    settle_output = to_sibling(output_own, lands_c[2])
     d_attended, d_query = upstream_rows[0], upstream_rows[1]
     d_attended[...] = matmul_right(d_branch[...], output_all[...].reshape(inner, width)).astype(BF16)
     send_off(7)
@@ -677,12 +672,14 @@
             pool[at, begin:begin + GROUP] = matmul_left(d_scores, stacked).astype(BF16)
             pool[at, inner + begin:inner + begin + GROUP] = matmul_left(probs.astype(BF16), upstream).astype(BF16)
 
-    pl.loop(0, 3)(attention_back_slot)
+    pl.loop(0, 2)(attention_back_slot)
+    pl.loop(0, 2)(output_grad_tile)
+    settle_output = to_sibling(output_own, lands_c[2])
+    pl.loop(2, 4)(attention_back_slot)
     settle_output()
     reductions.extend(halved_reduction(output_own, 4, output_result, 0, width, 8, 9, 10, 11))
     send_off(8)
-    pl.loop(3, slot_count)(attention_back_slot)
-    send_off(9)
+    pl.loop(4, slot_count)(attention_back_slot)
     block = width // length
 
     def query_grad_tile(zi):
@@ -703,11 +700,24 @@
             value = term if value is None else value + term
         up_all[zi] = value.astype(BF16).reshape(2, 2, block // 4, 2 * inner)
 
-    pl.loop(0, length)(context_grad_tile)
-    settle_context = to_sibling(context_own, lands_c[1])
-    settle_query()
-    reductions.extend(halved_reduction(query_own, 2, query_result, 0, inner, 10, 11, 12, 13))
-    settle_context()
+    context_moves = []
+
+    def settle_context(zi):
+        context_moves[zi].wait()
+        add_into(context_own(zi, ALL, ALL, rep), lands_c[1].at[zi])
+
+    for zi in range(length):
+        context_grad_tile(zi)
+        land = lands_c[1].at[zi]
+        context_moves.append(slots.move(links.device("core"), context_own(zi, ALL, ALL, 1 - rep), land, land))
+        context_moves[-1].start()
+        if zi == 1:
+            settle_query()
+            reductions.extend(halved_reduction(query_own, 2, query_result, 0, inner, 9, 10, 11, 12))
+            send_off(9)
+        if zi > 0:
+            settle_context(zi - 1)
+    settle_context(length - 1)
     reductions.extend(halved_reduction(context_own, 3, context_result, 0, inner, 10, 11, 12, 13))
     reductions.extend(halved_reduction(context_own, 3, context_result, inner, inner, 10, 12, 13, 14))
     send_off(10)
@@ -717,7 +727,7 @@
     after_back.near.wait()
     after_back.across.wait()
     slots.drain(5)
-    branch[:rows] = ((after[...] + after_lands[1].astype(F32) + after_lands[2].astype(F32)) * kept).astype(BF16)
+    branch[:rows] = ((after[...] + totals[1] + after_lands[1].astype(F32) + after_lands[2].astype(F32)) * kept).astype(BF16)
     written = [locals_.fill(
         [(branch.at[pl.ds(j * latent_count, latent_count)], latents_out.at[j]) for j in range(slot_count)], latents_out)]
 
@@ -758,7 +768,7 @@
             written.append(slots.move(links.device("core"), value, out.at[rep], out.at[1 - rep]))
             written[-1].start()
 
-    hand_over((0, 1))
+    hand_over((0, 1, 2, 4))
     pl.loop(3, slot_count)(input_slot)
     written.append(locals_.copy(media_in, media_grad_out))
     written.append(locals_.copy(latents_in, latents_grad_out))
@@ -769,7 +779,6 @@
     vector_sum.step(0)
     send_off(13)
     vector_sum.step(1)
-    hand_over((2, 4))
     vector_sum.step(2)
     send_off(14)
     hand_over((3,))
@@ -865,6 +874,45 @@
             collective_id=0, has_side_effects=True, vmem_limit_bytes=63 * 2 ** 20),
         name="resampler_layer",
     )(counts, media, latents, grad_out, packed, query_shard, context_shard, output_shard, up_shard, down_shard)
+
+
+def finish_kernel(length, latents_raw, media_grad_raw, latents_grad_raw, grads_raw, latents_out, media_grad_out,
+                  latents_grad_out, grads_out, local):
+    x = Links(length).x
+    locals_ = Locals(local)
+    count = media_grad_raw.shape[0]
+    copies = [locals_.fill([(media_grad_raw.at[j], media_grad_out.at[j]) for j in range(count)], media_grad_out)]
+    up, up_out = grads_raw[0], grads_out[0]
+    unit = grads_raw[1].shape[1]
+    moves = []
+    for core in range(2):
+        for plane in range(2):
+            half = x if plane == 0 else 1 - x
+            for owner in range(up.shape[-1] // unit):
+                begin = pl.multiple_of(((2 * owner + half) * 2 + core) * unit, unit)
+                moves.append((up.at[core, plane, :, pl.ds(owner * unit, unit)], up_out.at[:, pl.ds(begin, unit)]))
+    copies.append(locals_.fill(moves, up_out))
+    for raw, out in zip((latents_raw, latents_grad_raw) + tuple(grads_raw[1:]),
+                        (latents_out, latents_grad_out) + tuple(grads_out[1:])):
+        copies.append(locals_.copy(raw, out))
+    for copy in copies:
+        copy.wait()
+
+
+def finish(length, latents_raw, media_grad_raw, latents_grad_raw, grads_raw):
+    anywhere = pl.BlockSpec(memory_space=pl.ANY)
+    up = grads_raw[0]
+    shapes = [jax.ShapeDtypeStruct((up.shape[2], 4 * up.shape[3]), up.dtype)]
+    shapes += [jax.ShapeDtypeStruct(g.shape, g.dtype) for g in grads_raw[1:]]
+    same = [jax.ShapeDtypeStruct(r.shape, r.dtype) for r in (latents_raw, media_grad_raw, latents_grad_raw)]
+    return pl.pallas_call(
+        functools.partial(finish_kernel, length),
+        out_shape=(*same, shapes),
+        in_specs=[anywhere, anywhere, anywhere, [anywhere] * 5],
+        out_specs=(anywhere, anywhere, anywhere, [anywhere] * 5),
+        scratch_shapes=[pltpu.SemaphoreType.DMA((8,))],
+        name="finish",
+    )(latents_raw, media_grad_raw, latents_grad_raw, grads_raw)
 
 
 def head_scores(first_heads, second_heads):
@@ -1048,12 +1096,9 @@
         jnp.concatenate([jnp.where(side == 0, stacked, 0), jnp.where(side == 0, 0, stacked)], axis=1), ((0, 10), (0, 0)))
     latents_out, grad_media, grad_latents, vector_sums, summed = layer(
         chips // 4, image_counts, media[0], latents[0], grad_out[0], packed, weight_shards)
-    sums = [s.reshape(-1, s.shape[-1]) for s in summed[2:]]
-    rows, hidden = summed[0].shape[2:]
-    unit = summed[1].shape[1]
-    planes = jnp.where(lax.rem(lax.axis_index("dp"), 2) == 0, summed[0], summed[0][:, ::-1])
-    sums.append(planes.reshape(2, 2, rows, hidden // unit, unit).transpose(2, 3, 1, 0, 4).reshape(rows, 4 * hidden))
-    sums.append(summed[1].reshape(-1, summed[1].shape[-1]))
+    latents_out, grad_media, grad_latents, summed = finish(
+        chips // 4, latents_out, grad_media, grad_latents, summed)
+    sums = [s.reshape(-1, s.shape[-1]) for s in summed[2:] + summed[:2]]
     width = parameters[0].shape[0]
     mine = lax.dynamic_slice(vector_sums, (0, lax.axis_index("dp") * width), (6, width))
     return (latents_out[None], grad_media[None], grad_latents[None]) + tuple(mine) + tuple(sums)

time: 194 us -> 367 us (1.89)
  Pallas kernels: 176 us -> 363 us
  local copies, waits for them, and re-layouts: 13.3 us -> 2.05 us
    pallas_call x0 -> x1, Pallas kernels: none -> 200 us  [finish(): pl.pallas_call(functools.partial(finish_kernel, length), out_shape=(*same...]
    pallas_call x1, Pallas kernels: 176 us -> 163 us  [layer(): pl.pallas_call(functools.partial(layer_kernel, length, HEAD_DIM ** (-0.5)...]
    unnamed x20 -> x0, local copies, waits for them, and re-layouts: 8.65 us -> none
where the time goes in v4:
time: 367 us
  Pallas kernels  363 us (99%)
    pallas_call x1, Pallas kernels, finish(): pl.pallas_call(functools.partial(finish_kernel, length), out_shape=(*same...  200 us
    pallas_call x1, Pallas kernels, layer(): pl.pallas_call(functools.partial(layer_kernel, length, HEAD_DIM ** (-0.5)...  163 us

profile of v4, /device:TPU:0, one launch (start us, length us, event | category | flops | bytes accessed | tf_op | source)
XLA Modules:
  0.0 366.6 jit_solution(17261181470194474621)
XLA Ops:
  1.3 0.8 stack.27
  2.1 0.7 fusion.2.packed
  2.7 162.9 %resampler_layer.1 = (bf16[5,64,1024]{2,1,0:T(8,128)(2,1)}, bf16[5,256,1024]{2,1,0:T(8,128)(2,1)}, bf16[5,64,1024]{2,1,0:T(8,128)(2,1)}, f32[8,1024]{1,0:T(8,128...) custom-call(s32[1]{0:T(128)S(6)} %copy.29.counts, ...), custom_call_target="tpu_custom_call" | custom-call | tf_op jit(solution)/shard_map/resampler_layer/pallas_call | solution.py:867
  165.6 199.7 %finish.1 = (bf16[5,64,1024]{2,1,0:T(8,128)(2,1)}, bf16[5,256,1024]{2,1,0:T(8,128)(2,1)}, bf16[5,64,1024]{2,1,0:T(8,128)(2,1)}, f32[64,4096]{1,0:T(8,128)}, f32[...) custom-call(bf16[5,64,1024]{2,1,0:T(8,128)(2,1)} %get-tuple-element.31.latents_raw, ...), custom_call_target="tpu_custom_call" | custom-call | tf_op jit(solution)/shard_map/finish/pallas_call | solution.py:908
  365.4 0.8 constant_dynamic-slice_fusion
  366.1 0.5 slice_bitcast_fusion
  (1 shorter events, 0.0 us)

commit v5 on v4

--- a/solution.py
+++ b/solution.py
@@ -877,24 +877,33 @@
 
 
 def finish_kernel(length, latents_raw, media_grad_raw, latents_grad_raw, grads_raw, latents_out, media_grad_out,
-                  latents_grad_out, grads_out, local):
+                  latents_grad_out, grads_out, held, held_grads, local):
     x = Links(length).x
     locals_ = Locals(local)
+    raws = [latents_raw, latents_grad_raw, *grads_raw]
+    stages = [held[0], held[1], *held_grads]
+    outs = [latents_out, latents_grad_out, *grads_out]
     count = media_grad_raw.shape[0]
-    copies = [locals_.fill([(media_grad_raw.at[j], media_grad_out.at[j]) for j in range(count)], media_grad_out)]
-    up, up_out = grads_raw[0], grads_out[0]
+    for j in range(count):
+        raws.append(media_grad_raw.at[j])
+        stages.append(held[2].at[j])
+        outs.append(media_grad_out.at[j])
+    loads = [locals_.copy(raw, stage) for raw, stage in zip(raws, stages)]
     unit = grads_raw[1].shape[1]
-    moves = []
-    for core in range(2):
-        for plane in range(2):
-            half = x if plane == 0 else 1 - x
-            for owner in range(up.shape[-1] // unit):
-                begin = pl.multiple_of(((2 * owner + half) * 2 + core) * unit, unit)
-                moves.append((up.at[core, plane, :, pl.ds(owner * unit, unit)], up_out.at[:, pl.ds(begin, unit)]))
-    copies.append(locals_.fill(moves, up_out))
-    for raw, out in zip((latents_raw, latents_grad_raw) + tuple(grads_raw[1:]),
-                        (latents_out, latents_grad_out) + tuple(grads_out[1:])):
-        copies.append(locals_.copy(raw, out))
+    copies = []
+    for number, (load, stage, out) in enumerate(zip(loads, stages, outs)):
+        load.wait()
+        if number != 2:
+            copies.append(locals_.copy(stage, out))
+            continue
+        moves = []
+        for core in range(2):
+            for plane in range(2):
+                half = x if plane == 0 else 1 - x
+                for owner in range(stage.shape[-1] // unit):
+                    begin = pl.multiple_of(((2 * owner + half) * 2 + core) * unit, unit)
+                    moves.append((stage.at[core, plane, :, pl.ds(owner * unit, unit)], out.at[:, pl.ds(begin, unit)]))
+        copies.append(locals_.fill(moves, out))
     for copy in copies:
         copy.wait()
 
@@ -910,7 +919,12 @@
         out_shape=(*same, shapes),
         in_specs=[anywhere, anywhere, anywhere, [anywhere] * 5],
         out_specs=(anywhere, anywhere, anywhere, [anywhere] * 5),
-        scratch_shapes=[pltpu.SemaphoreType.DMA((8,))],
+        scratch_shapes=[
+            [pltpu.VMEM(r.shape, r.dtype) for r in (latents_raw, latents_grad_raw, media_grad_raw)],
+            [pltpu.VMEM(g.shape, g.dtype) for g in grads_raw],
+            pltpu.SemaphoreType.DMA((2 * (7 + media_grad_raw.shape[0]),)),
+        ],
+        compiler_params=pltpu.CompilerParams(vmem_limit_bytes=60 * 2 ** 20),
         name="finish",
     )(latents_raw, media_grad_raw, latents_grad_raw, grads_raw)
 

time: 367 us -> 173 us (0.47)
  Pallas kernels: 363 us -> 169 us
    pallas_call x1, Pallas kernels: 200 us -> 5.63 us  [finish(): pl.pallas_call(functools.partial(finish_kernel, length), out_shape=(*same...]
where the time goes in v5:
time: 173 us
  Pallas kernels  169 us (98%)
  local copies, waits for them, and re-layouts  2.05 us (1%)
    pallas_call x1, Pallas kernels, layer(): pl.pallas_call(functools.partial(layer_kernel, length, HEAD_DIM ** (-0.5)...  163 us
    pallas_call x1, Pallas kernels, finish(): pl.pallas_call(functools.partial(finish_kernel, length), out_shape=(*same...  5.63 us

profile of v5, /device:TPU:0, one launch (start us, length us, event | category | flops | bytes accessed | tf_op | source)
XLA Modules:
  0.0 172.6 jit_solution(4357331779907676804)
XLA Ops:
  1.3 0.8 stack.27
  2.1 0.7 fusion.2.packed
  2.7 162.9 %resampler_layer.1 = (bf16[5,64,1024]{2,1,0:T(8,128)(2,1)}, bf16[5,256,1024]{2,1,0:T(8,128)(2,1)}, bf16[5,64,1024]{2,1,0:T(8,128)(2,1)}, f32[8,1024]{1,0:T(8,128...) custom-call(s32[1]{0:T(128)S(6)} %copy.29.counts, ...), custom_call_target="tpu_custom_call" | custom-call | tf_op jit(solution)/shard_map/resampler_layer/pallas_call | solution.py:867
  165.6 5.6 %finish.1 = (bf16[5,64,1024]{2,1,0:T(8,128)(2,1)}, bf16[5,256,1024]{2,1,0:T(8,128)(2,1)}, bf16[5,64,1024]{2,1,0:T(8,128)(2,1)}, f32[64,4096]{1,0:T(8,128)}, f32[...) custom-call(bf16[5,64,1024]{2,1,0:T(8,128)(2,1)} %get-tuple-element.31.latents_raw, ...), custom_call_target="tpu_custom_call" | custom-call | tf_op jit(solution)/shard_map/finish/pallas_call | solution.py:917
  171.3 0.8 constant_dynamic-slice_fusion
  172.0 0.5 slice_bitcast_fusion
  (1 shorter events, 0.0 us)

commit v6 on v5

--- a/solution.py
+++ b/solution.py
@@ -316,9 +316,9 @@
 
 def layer_kernel(length, scaling, counts, media, latents, grad_out, packed, query_shard, context_shard,
                  output_shard, up_shard, down_shard, latents_out, media_grad_out, latents_grad_out, sums_out, grads_out,
-                 query_all, context_all, output_all, up_all, up_stage, down_all,
+                 query_all, context_all, output_all, up_all, down_all,
                  packed_all, vectors, media_in, latents_in, grad_in, context, key_value, query, attended, after,
-                 feed, feed_t, branch, branch_t, pool, totals, after_lands, d_feed_lands, upstream_rows,
+                 feed, feed_t, branch, branch_t, pool, totals, after_lands, d_feed_lands,
                  grad_up, grad_down, grad_query, grad_output, mask, sums, total, total_stage, total_lands,
                  own_rows_send, own_rows_land, lands_c, lands_b, lands_a, lands_z, result, send, recv, local):
     links = Links(length)
@@ -344,7 +344,8 @@
         staged.append(locals_.copy(shard.at[pl.ds(pl.multiple_of(rep * half, 16), half)], whole.at[z, y, x, rep]))
     units = range(hidden // unit)
     staged.append(locals_.fill(
-        [(up_shard.at[:, unit_columns(1 - x, n)], up_stage.at[:, pl.ds(n * unit, unit)]) for n in units], up_stage))
+        [(up_shard.at[:, unit_columns(1 - x, n)], own_rows_send.at[:, pl.ds(n * unit, unit)]) for n in units],
+        own_rows_send))
     staged.append(locals_.fill(
         [(up_shard.at[:, unit_columns(x, n)], up_all.at[z, y, x, :, pl.ds(n * unit, unit)]) for n in units],
         up_all.at[z, y, x]))
@@ -379,7 +380,7 @@
                 return up_all.at[zi, yi, ALL, :, window]
         ticks = (max(number - 1, 0), number + 2, number + 4)
         gathers.append((Gather(links, slots, view, ("z", "y"), False), ticks))
-    up_across = slots.move(links.device("x"), up_stage, up_all.at[z, y, x], up_all.at[z, y, 1 - x])
+    up_across = slots.move(links.device("x"), own_rows_send, up_all.at[z, y, x], up_all.at[z, y, 1 - x])
     slots.group = 3
     parts = [(0, 2 * latent_count), (2 * latent_count, rows - 2 * latent_count)]
     branch_rows = Rows(links, slots, branch, rows, [(0, rows)])
@@ -506,35 +507,17 @@
     feed_rows.near(0)
     feed_rows.near(1)
     slots.group = 6
-    for c in range(chunks):
-        begin = c * chunk
-        window = pl.ds(begin, chunk)
-        tiles(2, tall, lambda at, begin=begin: hidden_tile(at, begin))
-        if c == 0:
-            pump(9)
-            turn(feed, feed_t, 0)
-            feed_rows.forward(0)
-            feed_rows.forward(1)
-            feed_rows.far(0)
-            feed_rows.far(1)
-            turn(feed, feed_t, 2)
-        tiles(2, tall, lambda at, begin=begin: hidden_tile(pl.multiple_of(2 * rows + at, tall), begin))
-        if c == chunks - 1:
-            for group in range(1, 4):
-                slots.drain(group)
-            slots.group = 4
-            d_feed_back = Partials(links, slots, feed, d_feed_lands, rows)
-            slots.group = 5
-            after_back = Partials(links, slots, branch, after_lands, rows)
-            slots.group = 6
-            rounded(feed, 3, d_feed_of(3))
-            d_feed_back.far.start()
-            totals[1] = d_feed_of(2)
-            d_feed_back.far.wait()
-            across_tile(d_feed_back, feed)
-            d_feed_back.across.start()
-
-        def grad_tile(number, window=window, c=c):
+
+    def near_hidden(c):
+        tiles(2, tall, lambda at: hidden_tile(at, c * chunk))
+
+    def far_hidden(c):
+        tiles(2, tall, lambda at: hidden_tile(pl.multiple_of(2 * rows + at, tall), c * chunk))
+
+    def grads(c):
+        window = pl.ds(c * chunk, chunk)
+
+        def grad_tile(number):
             size = width // 2
             place = pl.multiple_of(number * size, size)
             up = matmul(feed_t[pl.ds(place, size)], d_hidden[:, window]).astype(BF16)
@@ -546,14 +529,46 @@
 
         pl.loop(0, 2)(grad_tile)
         reductions.append((plane_reduction(
-            lambda zi, yi, xi, window=window: grad_up.at[zi, yi, ALL, :, window],
+            lambda zi, yi, xi: grad_up.at[zi, yi, ALL, :, window],
             lands_b[0].at[:, :, :, window], lands_z[0].at[:, :, :, window],
-            functools.partial(keep_up, window=window)), (c, c + 3, c + 5)))
-        if c == 0:
-            pump(10)
-        if c == chunks - 2:
-            pump(11)
+            functools.partial(keep_up, window=window)), (c, c + 2, c + 4)))
         send_off(c)
+
+    near_hidden(0)
+    pump(9)
+    turn(feed, feed_t, 0)
+    feed_rows.forward(0)
+    feed_rows.forward(1)
+    feed_rows.far(0)
+    feed_rows.far(1)
+    turn(feed, feed_t, 2)
+    far_hidden(0)
+    grads(0)
+    near_hidden(1)
+    far_hidden(1)
+    pump(10)
+    near_hidden(2)
+    far_hidden(2)
+    grads(1)
+    for c in range(3, chunks):
+        pump(8 + c)
+        near_hidden(c)
+        far_hidden(c)
+    for group in range(1, 4):
+        slots.drain(group)
+    slots.group = 4
+    d_feed_back = Partials(links, slots, feed, d_feed_lands, rows)
+    slots.group = 5
+    after_back = Partials(links, slots, branch, after_lands, rows)
+    slots.group = 6
+    rounded(feed, 3, d_feed_of(3))
+    d_feed_back.far.start()
+    totals[1] = d_feed_of(2)
+    d_feed_back.far.wait()
+    across_tile(d_feed_back, feed)
+    d_feed_back.across.start()
+    for c in range(2, chunks):
+        grads(c)
     part_size = width // chunks
     for number in range(chunks):
         window = pl.ds(number * part_size, part_size)
@@ -564,7 +579,7 @@
         reductions.append((plane_reduction(
             lambda zi, yi, xi, window=window: grad_down.at[zi, yi, window],
             lands_b[1].at[:, window], lands_z[1].at[:, window], keep_down),
-            (chunks, chunks + 3 + number, chunks + 5 + number)))
+            (chunks, chunks + 2 + number, chunks + 4 + number) if number < chunks - 1 else (chunks, 10, 12)))
     send_off(4)
     rounded(feed, 1, d_feed_of(1))
     d_feed_back.near.start()
@@ -603,7 +618,6 @@
         feed[own] = d_middle.astype(BF16)
 
     tiles(slot_count, latent_count, middle_tile)
-    send_off(6)
 
     context_rows, output_rows = context_all.shape[-2], output_all.shape[-2]
 
@@ -626,9 +640,9 @@
 
         return settle
 
-    def halved_reduction(own, number, target, begin, size, *ticks):
+    def halved_reduction(own, number, target, begin, size, first, *ticks):
         made = []
-        for which, order in enumerate((("y", "x"), ("x", "y"))):
+        for which, order in enumerate((first, ("x", "y"))):
             window = pl.ds(begin + which * (size // 2), size // 2)
 
             def finish(value, window=window):
@@ -650,9 +664,9 @@
         grad_output[pl.ds(number * (length // 2), length // 2)] = value.reshape(
             length // 2, 2, 2, 2, output_rows, width)
 
-    d_attended, d_query = upstream_rows[0], upstream_rows[1]
-    d_attended[...] = matmul_right(d_branch[...], output_all[...].reshape(inner, width)).astype(BF16)
-    send_off(7)
+    d_attended, d_query = grad_in.at[:, :, pl.ds(0, inner)], grad_in.at[:, :, pl.ds(inner, inner)]
+    d_attended[...] = matmul_right(d_branch[...], output_all[...].reshape(inner, width)).astype(BF16).reshape(
+        slot_count, latent_count, inner)
 
     def attention_back_slot(j):
         own = pl.ds(pl.multiple_of(j * latent_count, latent_count), latent_count)
@@ -661,11 +675,11 @@
             values = key_value[j, :, inner + begin:inner + begin + GROUP]
             low_mask = mask[...].astype(BF16)
             stacked = spread_heads(query[j, :, begin:begin + GROUP], low_mask)
-            upstream = spread_heads(d_attended[own, begin:begin + GROUP], low_mask)
+            upstream = spread_heads(d_attended[j, :, begin:begin + GROUP], low_mask)
             probs = softmax(matmul_right(stacked, keys))
             d_probs = matmul_right(upstream, values)
             d_scores = (probs * (d_probs - jnp.sum(probs * d_probs, axis=-1, keepdims=True))).astype(BF16)
-            d_query[own, begin:begin + GROUP] = (
+            d_query[j, :, begin:begin + GROUP] = (
                 pick_heads(matmul(d_scores, keys), mask[...], latent_count).astype(BF16).astype(F32) * scaling
             ).astype(BF16)
             at = pl.ds(pl.multiple_of(j * key_count, 16), key_count)
@@ -673,19 +687,20 @@
             pool[at, inner + begin:inner + begin + GROUP] = matmul_left(probs.astype(BF16), upstream).astype(BF16)
 
     pl.loop(0, 2)(attention_back_slot)
+    send_off(6)
     pl.loop(0, 2)(output_grad_tile)
     settle_output = to_sibling(output_own, lands_c[2])
     pl.loop(2, 4)(attention_back_slot)
     settle_output()
-    reductions.extend(halved_reduction(output_own, 4, output_result, 0, width, 8, 9, 10, 11))
-    send_off(8)
+    reductions.extend(halved_reduction(output_own, 4, output_result, 0, width, ("x", "y"), 7, 9, 10, 11))
+    send_off(7)
     pl.loop(4, slot_count)(attention_back_slot)
     block = width // length
 
     def query_grad_tile(zi):
         place = pl.multiple_of(zi * block, block)
         turned = context[:, patches:, pl.ds(place, block)].reshape(rows, block).T
-        value = matmul(turned, d_query[...]).astype(BF16)
+        value = matmul(turned, d_query[...].reshape(rows, inner)).astype(BF16)
         grad_query[zi] = value.reshape(2, 2, 2, context_rows, inner)
 
     pl.loop(0, length)(query_grad_tile)
@@ -713,14 +728,14 @@
         context_moves[-1].start()
         if zi == 1:
             settle_query()
-            reductions.extend(halved_reduction(query_own, 2, query_result, 0, inner, 9, 10, 11, 12))
-            send_off(9)
+            reductions.extend(halved_reduction(query_own, 2, query_result, 0, inner, ("x", "y"), 8, 10, 11, 12))
+            send_off(8)
         if zi > 0:
             settle_context(zi - 1)
     settle_context(length - 1)
-    reductions.extend(halved_reduction(context_own, 3, context_result, 0, inner, 10, 11, 12, 13))
-    reductions.extend(halved_reduction(context_own, 3, context_result, inner, inner, 10, 12, 13, 14))
-    send_off(10)
+    reductions.extend(halved_reduction(context_own, 3, context_result, 0, inner, ("y", "x"), 9, 11, 12, 13))
+    reductions.extend(halved_reduction(context_own, 3, context_result, inner, inner, ("y", "x"), 9, 12, 13, 14))
+    send_off(9)
     slots.group = 7
     own_rows_move = slots.move(links.device("x"), own_rows_send, own_rows_land, own_rows_land)
     own_rows_move.start()
@@ -737,7 +752,7 @@
         at = pl.ds(pl.multiple_of(j * key_count, 16), key_count)
         own = pl.ds(pl.multiple_of(j * latent_count, latent_count), latent_count)
         context_up[...] = matmul_right(pool[at], context_all[...].reshape(width, 2 * inner))
-        context_up[patches:] = context_up[patches:] + matmul_right(d_query[own], query_all[...].reshape(width, inner))
+        context_up[patches:] = context_up[patches:] + matmul_right(d_query[j], query_all[...].reshape(width, inner))
 
         def media_tile(at, size=patches // 2):
             tile = pl.ds(at, size)
@@ -754,12 +769,24 @@
         sums[3] = sums[3] + fold(upstream)
         latents_in[j] = (d_feed[own] + value).astype(BF16)
 
-    pl.loop(0, 2)(input_slot)
+    pl.loop(0, 1)(input_slot)
+    send_off(10)
+    pl.loop(1, 3)(input_slot)
     send_off(11)
-    pl.loop(2, 3)(input_slot)
+    pl.loop(3, 4)(input_slot)
     send_off(12)
+    pl.loop(4, slot_count)(input_slot)
+    for number in range(6):
+        total[number:number + 1] = jnp.sum(sums[number], axis=0, keepdims=True)
+    total[6:] = jnp.zeros_like(total[6:])
+    vector_sum = VectorSum(links, slots, total, total_stage, total_lands)
+    vector_sum.step(0)
+    send_off(13)
+    written.append(locals_.copy(media_in, media_grad_out))
+    written.append(locals_.copy(latents_in, latents_grad_out))
     own_rows_move.wait()
     up_result[1] = own_rows_land[...].astype(F32)
+    vector_sum.step(1)
 
     def hand_over(numbers):
         for number in numbers:
@@ -769,21 +796,11 @@
             written[-1].start()
 
     hand_over((0, 1, 2, 4))
-    pl.loop(3, slot_count)(input_slot)
-    written.append(locals_.copy(media_in, media_grad_out))
-    written.append(locals_.copy(latents_in, latents_grad_out))
-    for number in range(6):
-        total[number:number + 1] = jnp.sum(sums[number], axis=0, keepdims=True)
-    total[6:] = jnp.zeros_like(total[6:])
-    vector_sum = VectorSum(links, slots, total, total_stage, total_lands)
-    vector_sum.step(0)
-    send_off(13)
-    vector_sum.step(1)
     vector_sum.step(2)
+    vector_sum.step(3)
+    vector_sum.step(4)
     send_off(14)
     hand_over((3,))
-    vector_sum.step(3)
-    vector_sum.step(4)
     sums_out[...] = total[...]
     for copy in written:
         copy.wait()
@@ -817,7 +834,6 @@
         pltpu.VMEM(halved(context_shard), BF16),
         pltpu.VMEM(halved(output_shard), BF16),
         pltpu.VMEM(up_shape, BF16),
-        pltpu.VMEM(up_shape[3:], BF16),
         pltpu.VMEM(down_shape, BF16),
         pltpu.VMEM(blocks + packed.shape, BF16),
         pltpu.VMEM((8, width), F32),
@@ -837,7 +853,6 @@
         pltpu.VMEM((2, rows, width), F32),
         pltpu.VMEM((3, rows, width), BF16),
         pltpu.VMEM((3, rows, width), BF16),
-        [pltpu.VMEM((rows, inner), BF16)] * 2,
         pltpu.VMEM(up_shape, BF16),
         pltpu.VMEM((length, 2, width, unit), BF16),
         pltpu.VMEM(halved(query_shard), BF16),
@@ -871,7 +886,7 @@
         out_specs=(anywhere, anywhere, anywhere, vmem, [anywhere] * 5),
         scratch_shapes=scratch,
         compiler_params=pltpu.CompilerParams(
-            collective_id=0, has_side_effects=True, vmem_limit_bytes=63 * 2 ** 20),
+            collective_id=0, has_side_effects=True, vmem_limit_bytes=127 * 2 ** 19),
         name="resampler_layer",
     )(counts, media, latents, grad_out, packed, query_shard, context_shard, output_shard, up_shard, down_shard)
 

time: 173 us -> 170 us (0.983)
  Pallas kernels: 169 us -> 165 us
    pallas_call x1, Pallas kernels: 163 us -> 160 us  [layer(): pl.pallas_call(functools.partial(layer_kernel, length, HEAD_DIM ** (-0.5)...]
where the time goes in v6:
time: 170 us; the launch traced here: 169 us
  Pallas kernels  165 us (97%)
  local copies, waits for them, and re-layouts  2.05 us (1%)
    pallas_call x1, Pallas kernels, layer(): pl.pallas_call(functools.partial(layer_kernel, length, HEAD_DIM ** (-0.5)...  160 us
    pallas_call x1, Pallas kernels, finish(): pl.pallas_call(functools.partial(finish_kernel, length), out_shape=(*same...  5.63 us

profile of v6, /device:TPU:0, one launch (start us, length us, event | category | flops | bytes accessed | tf_op | source)
XLA Modules:
  0.0 169.5 jit_solution(8729763234030561319)
XLA Ops:
  1.3 0.8 stack.27
  2.1 0.7 fusion.2.packed
  2.7 159.8 %resampler_layer.1 = (bf16[5,64,1024]{2,1,0:T(8,128)(2,1)}, bf16[5,256,1024]{2,1,0:T(8,128)(2,1)}, bf16[5,64,1024]{2,1,0:T(8,128)(2,1)}, f32[8,1024]{1,0:T(8,128...) custom-call(s32[1]{0:T(128)S(6)} %copy.29.counts, ...), custom_call_target="tpu_custom_call" | custom-call | tf_op jit(solution)/shard_map/resampler_layer/pallas_call | solution.py:882
  162.5 5.6 %finish.1 = (bf16[5,64,1024]{2,1,0:T(8,128)(2,1)}, bf16[5,256,1024]{2,1,0:T(8,128)(2,1)}, bf16[5,64,1024]{2,1,0:T(8,128)(2,1)}, f32[64,4096]{1,0:T(8,128)}, f32[...) custom-call(bf16[5,64,1024]{2,1,0:T(8,128)(2,1)} %get-tuple-element.31.latents_raw, ...), custom_call_target="tpu_custom_call" | custom-call | tf_op jit(solution)/shard_map/finish/pallas_call | solution.py:932
  168.2 0.8 constant_dynamic-slice_fusion
  168.9 0.5 slice_bitcast_fusion
  (1 shorter events, 0.0 us)

commit v7 on v6

--- a/solution.py
+++ b/solution.py
@@ -728,7 +728,7 @@
         context_moves[-1].start()
         if zi == 1:
             settle_query()
-            reductions.extend(halved_reduction(query_own, 2, query_result, 0, inner, ("x", "y"), 8, 10, 11, 12))
+            reductions.extend(halved_reduction(query_own, 2, query_result, 0, inner, ("y", "x"), 8, 10, 11, 12))
             send_off(8)
         if zi > 0:
             settle_context(zi - 1)
@@ -797,10 +797,10 @@
 
     hand_over((0, 1, 2, 4))
     vector_sum.step(2)
+    send_off(14)
+    hand_over((3,))
     vector_sum.step(3)
     vector_sum.step(4)
-    send_off(14)
-    hand_over((3,))
     sums_out[...] = total[...]
     for copy in written:
         copy.wait()

time: 170 us -> 169 us (level)
  no operation moved by 1% of the time
where the time goes in v7:
time: 169 us
  Pallas kernels  165 us (98%)
  local copies, waits for them, and re-layouts  2.05 us (1%)
    pallas_call x1, Pallas kernels, layer(): pl.pallas_call(functools.partial(layer_kernel, length, HEAD_DIM ** (-0.5)...  160 us
    pallas_call x1, Pallas kernels, finish(): pl.pallas_call(functools.partial(finish_kernel, length), out_shape=(*same...  5.63 us

profile of v7, /device:TPU:0, one launch (start us, length us, event | category | flops | bytes accessed | tf_op | source)
XLA Modules:
  0.0 169.3 jit_solution(8450690117716544816)
XLA Ops:
  1.3 0.8 stack.27
  2.1 0.7 fusion.2.packed
  2.7 159.6 %resampler_layer.1 = (bf16[5,64,1024]{2,1,0:T(8,128)(2,1)}, bf16[5,256,1024]{2,1,0:T(8,128)(2,1)}, bf16[5,64,1024]{2,1,0:T(8,128)(2,1)}, f32[8,1024]{1,0:T(8,128...) custom-call(s32[1]{0:T(128)S(6)} %copy.29.counts, ...), custom_call_target="tpu_custom_call" | custom-call | tf_op jit(solution)/shard_map/resampler_layer/pallas_call | solution.py:882
  162.3 5.6 %finish.1 = (bf16[5,64,1024]{2,1,0:T(8,128)(2,1)}, bf16[5,256,1024]{2,1,0:T(8,128)(2,1)}, bf16[5,64,1024]{2,1,0:T(8,128)(2,1)}, f32[64,4096]{1,0:T(8,128)}, f32[...) custom-call(bf16[5,64,1024]{2,1,0:T(8,128)(2,1)} %get-tuple-element.31.latents_raw, ...), custom_call_target="tpu_custom_call" | custom-call | tf_op jit(solution)/shard_map/finish/pallas_call | solution.py:932
  168.0 0.8 constant_dynamic-slice_fusion
  168.7 0.5 slice_bitcast_fusion
  (1 shorter events, 0.0 us)

commit v8 on v7

--- a/solution.py
+++ b/solution.py
@@ -734,7 +734,7 @@
             settle_context(zi - 1)
     settle_context(length - 1)
     reductions.extend(halved_reduction(context_own, 3, context_result, 0, inner, ("y", "x"), 9, 11, 12, 13))
-    reductions.extend(halved_reduction(context_own, 3, context_result, inner, inner, ("y", "x"), 9, 12, 13, 14))
+    reductions.extend(halved_reduction(context_own, 3, context_result, inner, inner, ("y", "x"), 9, 11, 12, 13))
     send_off(9)
     slots.group = 7
     own_rows_move = slots.move(links.device("x"), own_rows_send, own_rows_land, own_rows_land)

time: 169 us -> 172 us (1.018)
  Pallas kernels: 165 us -> 168 us
    pallas_call x1, Pallas kernels: 160 us -> 162 us  [layer(): pl.pallas_call(functools.partial(layer_kernel, length, HEAD_DIM ** (-0.5)...]
where the time goes in v8:
time: 172 us
  Pallas kernels  168 us (98%)
  local copies, waits for them, and re-layouts  2.05 us (1%)
    pallas_call x1, Pallas kernels, layer(): pl.pallas_call(functools.partial(layer_kernel, length, HEAD_DIM ** (-0.5)...  162 us
    pallas_call x1, Pallas kernels, finish(): pl.pallas_call(functools.partial(finish_kernel, length), out_shape=(*same...  5.63 us

profile of v8, /device:TPU:0, one launch (start us, length us, event | category | flops | bytes accessed | tf_op | source)
XLA Modules:
  0.0 171.7 jit_solution(14637716718064539731)
XLA Ops:
  1.3 0.8 stack.27
  2.1 0.7 fusion.2.packed
  2.7 162.0 %resampler_layer.1 = (bf16[5,64,1024]{2,1,0:T(8,128)(2,1)}, bf16[5,256,1024]{2,1,0:T(8,128)(2,1)}, bf16[5,64,1024]{2,1,0:T(8,128)(2,1)}, f32[8,1024]{1,0:T(8,128...) custom-call(s32[1]{0:T(128)S(6)} %copy.29.counts, ...), custom_call_target="tpu_custom_call" | custom-call | tf_op jit(solution)/shard_map/resampler_layer/pallas_call | solution.py:882
  164.8 5.6 %finish.1 = (bf16[5,64,1024]{2,1,0:T(8,128)(2,1)}, bf16[5,256,1024]{2,1,0:T(8,128)(2,1)}, bf16[5,64,1024]{2,1,0:T(8,128)(2,1)}, f32[64,4096]{1,0:T(8,128)}, f32[...) custom-call(bf16[5,64,1024]{2,1,0:T(8,128)(2,1)} %get-tuple-element.31.latents_raw, ...), custom_call_target="tpu_custom_call" | custom-call | tf_op jit(solution)/shard_map/finish/pallas_call | solution.py:932
  170.4 0.8 constant_dynamic-slice_fusion
  171.1 0.5 slice_bitcast_fusion
  (1 shorter events, 0.0 us)
